TPU v7x, 32 devices: a whole 2x2x4 slice. The times are simulated.
32 devices in a mesh: lat: 4 (over x, core), lon: 8 (over z, y).
Axes of the slice: x: 2, y: 2, z: 4, core: 2. Of those that a mesh axis runs over, the one named last changes fastest.
Arguments:
- fields: bfloat16 [512, 1440, 256], P('lat', 'lon'), may hold values from -6 to 6
- basis: float32 [512, 4, 3, 17], P('lat'), may hold values from -1 to 1
- reach: int32 [512], P('lat'), may hold values from 1 to 8, as said below
- mixing: bfloat16 [4, 256, 256], replicated, may hold values from -0.1875 to 0.1875
- gains: float32 [2, 720, 256], replicated, may hold values from -5 to 5
Outputs:
- updated: bfloat16 [512, 1440, 256], P('lat', 'lon')
Inputs may be any that keep to these rules, and one draw needn't show every extreme that they name: `reach`: 8 is reached in some row.
All inputs are finite; a program needn't handle non-finite values.
Results may differ from a plain program's by a relative error of at most 0.0062.
Values may be sent and summed in bfloat16 or wider, within the bound.
A program may use at most 576 MiB of HBM per device.

v0:
```python
import jax
import jax.numpy as jnp
from jax import lax
from jax.sharding import PartitionSpec as P

NLON = 1440
MODES = 720
HALO = 8
WIN = 17


def with_halo(block, sides, width, periodic):
    for axis, dim in sides:
        count = lax.axis_size(axis)
        forward = [(i, i + 1) for i in range(count - 1)]
        if periodic:
            forward.append((count - 1, 0))
        backward = [(target, source) for source, target in forward]
        low = lax.ppermute(
            lax.slice_in_dim(block, block.shape[dim] - width, None, axis=dim), axis, forward
        )
        high = lax.ppermute(lax.slice_in_dim(block, 0, width, axis=dim), axis, backward)
        block = jnp.concatenate([low, block, high], axis=dim)
    return block


def make_tables(count, modes):
    index = jnp.arange(count, dtype=jnp.int32)
    wave = jnp.arange(modes, dtype=jnp.int32)
    phase = index[:, None] * wave[None, :] % count
    angle = phase.astype(jnp.float32) * (2.0 * jnp.pi / count)
    cosine = jnp.cos(angle)
    sine = jnp.sin(angle)
    forward = jnp.concatenate([cosine, -sine], 1)
    weights = jnp.where(wave == 0, 1.0, 2.0).astype(jnp.float32) / count
    weights = jnp.concatenate([weights, weights], 0)
    adjoint = forward * weights[None, :]
    return (forward.astype(jnp.bfloat16), adjoint.astype(jnp.bfloat16))


def transform(piece, forward, adjoint, gain_real, gain_imag):
    spectrum = jnp.einsum("rnc,nf->rfc", piece, forward, preferred_element_type=jnp.float32)
    real = spectrum[:, :MODES]
    imag = spectrum[:, MODES:]
    filtered = jnp.concatenate(
        [gain_real * real - gain_imag * imag, gain_real * imag + gain_imag * real], 1
    ).astype(jnp.bfloat16)
    return jnp.einsum("rfc,nf->rnc", filtered, adjoint, preferred_element_type=jnp.float32).astype(
        jnp.bfloat16
    )


def shards(fields, basis, reach, mixing, gains):
    lat_rows, lon_cols, chans = fields.shape
    wide = with_halo(fields, (("lon", 1),), HALO, True)
    padded = with_halo(wide, (("lat", 0),), 1, False)
    offsets = jnp.arange(WIN, dtype=jnp.int32) - HALO
    mask = (jnp.abs(offsets)[None, :] <= reach[:, None]).astype(jnp.float32)
    filters = (basis * mask[:, None, None, :]).astype(jnp.bfloat16)
    target = jnp.arange(lon_cols, dtype=jnp.int32)
    source = jnp.arange(lon_cols + 2 * HALO, dtype=jnp.int32)
    select = (
        source[None, :, None] - target[:, None, None] == offsets[None, None, :] + HALO
    ).astype(jnp.bfloat16)
    band = jnp.einsum(
        "ikab,jpb->ikjap", filters, select, preferred_element_type=jnp.float32
    ).astype(jnp.bfloat16)
    windows = jnp.stack([padded[0:lat_rows], padded[1 : lat_rows + 1], padded[2 : lat_rows + 2]], 1)
    conv = jnp.einsum("ikjap,iapc->ikjc", band, windows, preferred_element_type=jnp.float32).astype(
        jnp.bfloat16
    )
    local = jnp.einsum("ikjc,kcd->ijd", conv, mixing, preferred_element_type=jnp.float32)
    forward, adjoint = make_tables(NLON, MODES)
    gathered = lax.all_to_all(fields, "lon", split_axis=0, concat_axis=1, tiled=True)
    result = transform(gathered, forward, adjoint, gains[0], gains[1])
    back = lax.all_to_all(result, "lon", split_axis=1, concat_axis=0, tiled=True)
    return (fields.astype(jnp.float32) + local + back.astype(jnp.float32)).astype(jnp.bfloat16)


def solution(mesh):
    return jax.shard_map(
        shards,
        mesh=mesh,
        in_specs=(P("lat", "lon", None), P("lat", None, None, None), P("lat"), P(), P()),
        out_specs=P("lat", "lon", None),
        check_vma=False,
    )
```

profile of v0, /device:TPU:13, one launch (start us, length us, event | category | flops | bytes accessed | tf_op | source)
XLA Modules:
  0.0 1040.3 jit_solution(17651418187520683294)
XLA Ops:
  0.0 0.0 copy-start
  0.0 13.9 %copy.26 = bf16[128,180,256]{2,1,0:T(8,128)(2,1)} copy(bf16[128,180,256]{2,0,1:T(8,128)(2,1)} %param.5) | data formatting | bytes 23592960 | tf_op args[0]
  13.9 5.8 all-to-all-start
  19.7 0.1 pad_maximum_fusion.8
  19.7 1.0 slice_bitcast_fusion.1
  20.7 19.7 %sine_negate_fusion = (f32[1440,720]{0,1:T(8,128)}, f32[1440,720]{0,1:T(8,128)}) fusion(), kind=kLoop, calls=%fused_computation.40 | loop fusion | flops 10368000 | bytes 8294400 | tf_op jit(solution)/shard_map/neg | solution.py:34
  40.4 238.4 %all-to-all-done = bf16[128,180,256]{2,1,0:T(8,128)(2,1)} async-done(((bf16[128,180,256]{2,1,0:T(8,128)(2,1)}), bf16[128,180,256]{2,1,0:T(8,128)(2,1)}, u32[]{:S(2)}, u32[]{:S(2)}) %all-to-all-start) | async-done | bytes 11796512 | tf_op jit(solution)/shard_map/all_to_all | solution.py:74
  278.8 13.4 %copy.36 = bf16[16,8,180,256]{3,0,2,1:T(8,128)(2,1)S(1)} copy(bf16[16,8,180,256]{3,2,0,1:T(8,128)(2,1)} %bitcast.21) | data formatting | bytes 23592960 | tf_op jit(solution)/shard_map/all_to_all | solution.py:74
  292.2 27.4 %convolution_bitcast_fusion = f32[16,1440,256]{2,1,0:T(8,128)} fusion(bf16[16,1440,256]{2,0,1:T(8,128)(2,1)S(1)} %bitcast.85, f32[1440,720]{0,1:T(8,128)S(1)} %bitcast.87, f32[1440,720]{0,1:T(8,128)} %get-tuple-element.17), kind=kOutput, calls=%fused_computation.13 | convolution fusion | flops 16995225600 | bytes 43683840 | tf_op jit(solution)/shard_map/rnc,nf->rfc/dot_general | solution.py:42
  319.6 14.0 %subtract_convert_fusion = (bf16[16,720,256]{2,1,0:T(8,128)(2,1)}, bf16[16,720,256]{2,1,0:T(8,128)(2,1)}) fusion(f32[16,1440,256]{2,1,0:T(8,128)} %convolution_bitcast_fusion, f32[720,256]{1,0:T(8,128)} %get-tuple-element.15, f32[720,256]{1,0:T(8,128)S(1)} %get-tuple-element.14), kind=kLoop, calls=%fused_computation.29 | loop fusion | flops 23592960 | bytes 36864000 | tf_op jit(solution)/shard_map/convert.3
  333.6 24.5 %fusion.13 = bf16[16,1440,256]{2,1,0:T(8,128)(2,1)S(1)} fusion(bf16[16,720,256]{2,1,0:T(8,128)(2,1)} %get-tuple-element.6, bf16[16,720,256]{2,1,0:T(8,128)(2,1)} %get-tuple-element.5, f32[1440,720]{0,1:T(8,128)} %get-tuple-element.16, f32[1440,720]{0,1:T(8,128)} %get-tuple-element.17, f32[1440]{0:T(1024)S(1)} %pad_maximum_fusion.8), kind=kOutput, calls=%fused_computation.30 | convolution fusion | flops 17022643200 | bytes 31893120 | tf_op jit(solution)/shard_map/rfc,nf->rnc/dot_general | solution.py:48
  358.1 28.1 %copy.39 = bf16[16,1440,256]{2,0,1:T(8,128)(2,1)} copy(bf16[16,1440,256]{2,1,0:T(8,128)(2,1)S(1)} %fusion.13) | data formatting | bytes 23592960 | tf_op jit(solution)/shard_map/convert_element_type | solution.py:48
  386.2 7.1 all-to-all-start.1
  393.2 1.5 fusion.41
  394.8 0.3 collective-permute-start.1
  395.1 2.1 collective-permute-start
  397.2 0.1 compare_convert_fusion
  397.3 260.3 %collective-permute-done.1 = bf16[128,8,256]{2,1,0:T(8,128)(2,1)S(1)} collective-permute-done((bf16[128,8,256]{2,1,0:T(8,128)(2,1)S(1)}, bf16[128,8,256]{2,1,0:T(8,128)(2,1)S(1)}, u32[]{:S(2)}, u32[]{:S(2)}) %collective-permute-start.1) | collective-permute-done | bytes 524320 | tf_op jit(solution)/shard_map/ppermute | solution.py:22
  657.6 0.1 collective-permute-done
  657.8 7.1 pad_maximum_fusion.6
  664.9 5.6 collective-permute-start.2
  670.5 1.9 collective-permute-start.3
  672.4 39.6 %convert_bitcast_fusion = bf16[128,4,180,3,196]{0,4,3,1,2:T(8,128)(2,1)} fusion(s32[180,196]{1,0:T(8,128)S(1)} %iota_subtract_fusion, bf16[128,4,3,17]{0,1,3,2:T(4,128)(2,1)S(1)} %multiply_convert_fusion.1), kind=kOutput, calls=%fused_computation | convolution fusion | flops 1897252608 | bytes 108573504 | tf_op jit(solution)/shard_map/ikab,jpb->ikjap/dot_general | solution.py:65
  712.0 174.6 %copy.33 = bf16[128,4,180,3,196]{4,2,3,1,0:T(8,128)(2,1)} copy(bf16[128,4,180,3,196]{0,4,3,1,2:T(8,128)(2,1)} %convert_bitcast_fusion) | data formatting | bytes 216760320 | tf_op jit(solution)/shard_map/convert_element_type | solution.py:67
  886.6 0.0 collective-permute-done.2
  886.6 0.0 collective-permute-done.3
  886.6 32.2 %fusion.8 = (bf16[128,1,196,256]{3,2,1,0:T(8,128)(2,1)}, bf16[128,1,196,256]{3,2,1,0:T(8,128)(2,1)}, bf16[128,1,196,256]{3,2,1,0:T(8,128)(2,1)}) fusion(bf16[1,196,256]{2,1,0:T(8,128)(2,1)S(1)} %collective-permute-done.2, bf16[128,8,256]{2,1,0:T(8,128)(2,1)S(1)} %collective-permute-done.1, bf16[128,180,256]{2,1,0:T(8,128)(2,1)} %copy.26, ...), kind=kLoop, calls=%fused_computation.20 | loop fusion | flops 141295616 | bytes 51580928 | tf_op jit(solution)/shard_map/stack | solution.py:68
  918.8 0.0 all-to-all-done.1
  918.8 7.1 convert_bitcast_fusion.1
  925.9 16.6 %copy.40 = f32[8,16,180,256]{3,2,1,0:T(8,128)} copy(f32[8,16,180,256]{3,1,2,0:T(8,128)S(1)} %convert_bitcast_fusion.1) | data formatting | bytes 47185920 | tf_op jit(solution)/shard_map/convert_element_type | solution.py:77
  942.5 81.1 %fusion.6 = bf16[128,180,256]{2,1,0:T(8,128)(2,1)} fusion(f32[8,16,180,256]{3,2,1,0:T(8,128)} %copy.40, bf16[128,4,180,3,196]{4,2,3,1,0:T(8,128)(2,1)} %copy.33, bf16[128,1,196,256]{3,2,1,0:T(8,128)(2,1)} %get-tuple-element.9, bf16[128,1,196,256]{3,2,1,0:T(8,128)(2,1)} %get-tuple-element.8, bf16[128,1,196,256]{3,2,1,0:T(8,128)(2,1)} %get-tuple-element.7, ...), kind=kOutput, calls=%fused_computation.10 | convolution fusion | flops 39910637568 | bytes 194625536 | tf_op jit(solution)/shard_map/ikjc,kcd->ijd/dot_general | solution.py:72
  1023.7 16.1 %copy.41 = bf16[128,180,256]{2,0,1:T(8,128)(2,1)} copy(bf16[128,180,256]{2,1,0:T(8,128)(2,1)} %fusion.6) | data formatting | bytes 23592960 | tf_op jit(solution)/shard_map/convert_element_type | solution.py:77
  (17 shorter events, 0.1 us)
Async XLA Ops:
  0.0 942.5 %copy-start = (bf16[4,256,256]{2,1,0:T(8,128)(2,1)S(1)}, bf16[4,256,256]{2,1,0:T(8,128)(2,1)}, u32[]{:S(2)}) copy-start(bf16[4,256,256]{2,1,0:T(8,128)(2,1)} %param.8) | copy-start | bytes 1572868
  13.9 5.9 copy-start.1
  13.9 265.0 %all-to-all-start = ((bf16[128,180,256]{2,1,0:T(8,128)(2,1)}), bf16[128,180,256]{2,1,0:T(8,128)(2,1)}, u32[]{:S(2)}, u32[]{:S(2)}) async-start(bf16[128,180,256]{2,1,0:T(8,128)(2,1)} %copy.26), calls=%async_computation | async-start | bytes 24117248 | tf_op jit(solution)/shard_map/all_to_all | solution.py:74
  40.4 251.8 %slice-start = ((s8[4423680]{0:T(1024)(128)(4,1)}), s8[229376]{0:T(1024)(128)(4,1)S(1)}, s32[]{:S(2)}) async-start(s8[4423680]{0:T(1024)(128)(4,1)} %bitcast.86), calls=%async_computation.2 | async-start | bytes 458752
  278.8 13.4 %slice-start.1 = ((s8[4423680]{0:T(1024)(128)(4,1)}), s8[4194304]{0:T(1024)(128)(4,1)S(1)}, s32[]{:S(2)}) async-start(s8[4423680]{0:T(1024)(128)(4,1)} %bitcast.86), calls=%async_computation.3 | async-start | bytes 8388608
  386.2 11.0 %copy-start.3 = (s32[128]{0:T(128)S(1)}, s32[128]{0:T(128)}, u32[]{:S(2)}) copy-start(s32[128]{0:T(128)} %param.7) | copy-start | bytes 1540
  386.2 11.1 %copy-start.2 = (f32[128,4,3,17]{0,1,3,2:T(4,128)S(1)}, f32[128,4,3,17]{0,1,3,2:T(4,128)}, u32[]{:S(2)}) copy-start(f32[128,4,3,17]{0,1,3,2:T(4,128)} %param.6) | copy-start | bytes 313348
  386.2 532.6 %all-to-all-start.1 = ((bf16[16,1440,256]{2,0,1:T(8,128)(2,1)}), bf16[16,1440,256]{2,0,1:T(8,128)(2,1)}, u32[]{:S(2)}, u32[]{:S(2)}) async-start(bf16[16,1440,256]{2,0,1:T(8,128)(2,1)} %copy.39), calls=%async_computation.1 | async-start | bytes 23592960 | tf_op jit(solution)/shard_map/all_to_all | solution.py:76
  394.8 262.9 %collective-permute-start.1 = (bf16[128,8,256]{2,1,0:T(8,128)(2,1)S(1)}, bf16[128,8,256]{2,1,0:T(8,128)(2,1)S(1)}, u32[]{:S(2)}, u32[]{:S(2)}) collective-permute-start(bf16[128,8,256]{2,1,0:T(8,128)(2,1)S(1)} %get-tuple-element.13), channel_id=1, source_target_pairs={{1,0},{2,1},{3,2},{4,3},{5,4},{6,5},{7,6},{0,7},{9,8},{10,9},{11,1... | collective-permute-start | bytes 1572872 | tf_op jit(solution)/shard_map/ppermute | solution.py:22
  395.1 262.7 %collective-permute-start = (bf16[128,8,256]{2,1,0:T(8,128)(2,1)S(1)}, bf16[128,8,256]{2,1,0:T(8,128)(2,1)S(1)}, u32[]{:S(2)}, u32[]{:S(2)}) collective-permute-start(bf16[128,8,256]{2,1,0:T(8,128)(2,1)S(1)} %get-tuple-element.12), channel_id=1, source_target_pairs={{0,1},{1,2},{2,3},{3,4},{4,5},{5,6},{6,7},{7,0},{8,9},{9,10},{10,1... | collective-permute-start | bytes 1572872 | tf_op jit(solution)/shard_map/ppermute | solution.py:19
  664.9 221.7 %collective-permute-start.2 = (bf16[1,196,256]{2,1,0:T(8,128)(2,1)S(1)}, bf16[1,196,256]{2,1,0:T(8,128)(2,1)S(1)}, u32[]{:S(2)}, u32[]{:S(2)}) collective-permute-start(bf16[1,196,256]{2,1,0:T(8,128)(2,1)S(1)} %get-tuple-element.10), channel_id=1, source_target_pairs={{0,8},{8,16},{16,24},{1,9},{9,17},{17,25},{2,10},{10,18},{18,26},{... | collective-permute-start | bytes 301064 | tf_op jit(solution)/shard_map/ppermute | solution.py:19
  670.5 216.1 %collective-permute-start.3 = (bf16[1,196,256]{2,1,0:T(8,128)(2,1)S(1)}, bf16[1,196,256]{2,1,0:T(8,128)(2,1)S(1)}, u32[]{:S(2)}, u32[]{:S(2)}) collective-permute-start(bf16[1,196,256]{2,1,0:T(8,128)(2,1)S(1)} %get-tuple-element.11), channel_id=1, source_target_pairs={{8,0},{16,8},{24,16},{9,1},{17,9},{25,17},{10,2},{18,10},{26,18},{... | collective-permute-start | bytes 301064 | tf_op jit(solution)/shard_map/ppermute | solution.py:22
where the time goes:
time: 1050 us; the launch traced here: 1040 us
  waiting for transfers between devices  499 us (48%)
  local copies, waits for them, and re-layouts  265 us (25%)
  matrix products  173 us (16%)
  other arithmetic  80.3 us (8%)
  starting transfers between devices  22.8 us (2%)
    ppermute x2, waiting for transfers between devices, with_halo(): lax.ppermute(lax.slice_in_dim(block, 0, width, axis=dim), axis, backward)  260 us
    all_to_all x1, waiting for transfers between devices, shards(): lax.all_to_all(fields, 'lon', split_axis=0, concat_axis=1, tiled=True)  238 us
    convert_element_type x1, local copies, waits for them, and re-layouts, shards(): band = jnp.einsum('ikab,jpb->ikjap', filters, select, preferred_element_t...  175 us
    dot_general x1, matrix products, shards(): jnp.einsum('ikjc,kcd->ijd', conv, mixing, preferred_element_type=jnp.floa...  81.1 us
    dot_general x1, matrix products, shards(): jnp.einsum('ikab,jpb->ikjap', filters, select, preferred_element_type=jnp...  39.6 us
    another operation x1, other arithmetic, shards(): jnp.stack([padded[0:lat_rows], padded[1:lat_rows + 1], padded[2:lat_rows...  32.2 us
    convert_element_type x1, local copies, waits for them, and re-layouts, transform(): jnp.einsum('rfc,nf->rnc', filtered, adjoint, preferred_element_type=jnp.f...  28.1 us
    dot_general x1, matrix products, transform(): jnp.einsum('rnc,nf->rfc', piece, forward, preferred_element_type=jnp.floa...  27.4 us
  transfers between devices with their start and end apart: 6, of which 3 were waited for; matrix products, arithmetic and copies ran while one was open for 27% of the time, Pallas kernels for 0%

commit v1 on v0

v1 whole, which is shorter than its diff:
```python
import functools

import jax
import jax.numpy as jnp
from jax import lax
from jax.experimental import pallas as pl
from jax.experimental.pallas import tpu as pltpu
from jax.sharding import PartitionSpec as P

NLON = 1440
MODES = 720
HALO = 8
WIN = 17
TILE = 64
SPAN = TILE + 2 * HALO
GROUP = 4
PARTS = 2
LIMIT = 48 * 1024 * 1024


def exchange(block, axis, dim, width, periodic):
    count = lax.axis_size(axis)
    forward = [(i, i + 1) for i in range(count - 1)]
    if periodic:
        forward.append((count - 1, 0))
    backward = [(target, source) for source, target in forward]
    low = lax.ppermute(
        lax.slice_in_dim(block, block.shape[dim] - width, None, axis=dim), axis, forward
    )
    high = lax.ppermute(lax.slice_in_dim(block, 0, width, axis=dim), axis, backward)
    return low, high


def tables(count, cols):
    wave = jnp.arange(MODES, dtype=jnp.int32)

    def phases(index):
        phase = index * wave % NLON
        return phase.astype(jnp.float32) * (2.0 * jnp.pi / NLON)

    index = jnp.arange(NLON, dtype=jnp.int32)
    angle = phases(index[:, None])
    forward = jnp.concatenate([jnp.cos(angle), -jnp.sin(angle)], 1)
    weights = jnp.where(wave == 0, 1.0, 2.0).astype(jnp.float32) / NLON
    weights = jnp.concatenate([weights, weights], 0)
    adjoint = (forward * weights[None, :]).astype(jnp.bfloat16)
    forward = forward.astype(jnp.bfloat16).reshape(count, cols, 2 * MODES)
    rows = -(-cols // 8) * 8
    adjoint = jnp.pad(adjoint.reshape(count, cols, 2 * MODES), ((0, 0), (0, rows - cols), (0, 0)))
    return forward.transpose(0, 2, 1), adjoint.reshape(count * rows, 2 * MODES)


def transform_kernel(count, cols, rows, x_ref, f_ref, a_ref, g_ref, o_ref, filtered):
    step = 240
    for at in range(0, MODES, step):
        real = jnp.zeros((step, x_ref.shape[-1]), jnp.float32)
        imag = real
        for s in range(count):
            x = x_ref[s, 0]
            real += jnp.dot(f_ref[s, at : at + step], x, preferred_element_type=jnp.float32)
            imag += jnp.dot(
                f_ref[s, MODES + at : MODES + at + step], x, preferred_element_type=jnp.float32
            )
        gain_real = g_ref[0, at : at + step]
        gain_imag = g_ref[1, at : at + step]
        filtered[at : at + step] = (gain_real * real - gain_imag * imag).astype(jnp.bfloat16)
        filtered[MODES + at : MODES + at + step] = (gain_real * imag + gain_imag * real).astype(
            jnp.bfloat16
        )
    back = jnp.dot(a_ref[...], filtered[...], preferred_element_type=jnp.float32)
    for s in range(count):
        o_ref[s, 0] = back[s * rows : s * rows + cols].astype(jnp.bfloat16)


def transform(piece, forward, adjoint, gains):
    count, height, cols, chans = piece.shape
    rows = -(-cols // 8) * 8
    block = pl.BlockSpec((count, 1, cols, chans), lambda r: (0, r, 0, 0))
    return pl.pallas_call(
        functools.partial(transform_kernel, count, cols, rows),
        grid=(height,),
        in_specs=[
            block,
            pl.BlockSpec(forward.shape, lambda r: (0, 0, 0)),
            pl.BlockSpec(adjoint.shape, lambda r: (0, 0)),
            pl.BlockSpec(gains.shape, lambda r: (0, 0, 0)),
        ],
        out_specs=block,
        out_shape=jax.ShapeDtypeStruct(piece.shape, jnp.bfloat16),
        scratch_shapes=[pltpu.VMEM((2 * MODES, chans), jnp.bfloat16)],
        compiler_params=pltpu.CompilerParams(vmem_limit_bytes=LIMIT),
        cost_estimate=pl.CostEstimate(
            flops=height * 4 * 2 * MODES * NLON * chans,
            bytes_accessed=4 * piece.size + 12_000_000,
            transcendentals=0,
        ),
        name="transform",
    )(piece, forward, adjoint, gains)


def local_kernel(tiles, w_ref, n0_ref, n1_ref, taps_ref, mix_ref, x_ref, o_ref, conv):
    basis_count = taps_ref.shape[1]
    chans = x_ref.shape[-1]
    cols = x_ref.shape[1]
    height = tiles * TILE
    zeros = jnp.zeros((256 - 3 * SPAN, chans), jnp.bfloat16)
    for r in range(GROUP):
        bands = []
        for k in range(basis_count):
            row = jnp.broadcast_to(taps_ref[r, k : k + 1], (TILE, 256))
            bands.append(pltpu.roll(row, 0, 1, stride=1, stride_axis=0).astype(jnp.bfloat16))
        band = jnp.concatenate(bands, 0)
        for t in range(tiles):
            at = slice(t * TILE, t * TILE + SPAN)
            pieces = []
            for a in range(3):
                if r + a < GROUP:
                    pieces.append(w_ref[r + a, at])
                elif r + a == GROUP:
                    pieces.append(n0_ref[0, at])
                else:
                    pieces.append(n1_ref[0, at])
            window = jnp.concatenate(pieces + [zeros], 0)
            out = jnp.dot(band, window, preferred_element_type=jnp.float32).astype(jnp.bfloat16)
            at = r * height + t * TILE
            for k in range(basis_count):
                conv[k, at : at + TILE] = out[k * TILE : (k + 1) * TILE]
    total = jnp.dot(conv[0], mix_ref[0], preferred_element_type=jnp.float32)
    for k in range(1, basis_count):
        total += jnp.dot(conv[k], mix_ref[k], preferred_element_type=jnp.float32)
    for r in range(GROUP):
        mixed = total[r * height : r * height + cols]
        o_ref[r] = (x_ref[r].astype(jnp.float32) + mixed).astype(jnp.bfloat16)


def local_part(fields, padded, taps, mixing):
    lat_rows, cols, chans = fields.shape
    wide = padded.shape[1]
    tiles = (wide - 2 * HALO) // TILE
    basis_count = mixing.shape[0]
    block = pl.BlockSpec((GROUP, cols, chans), lambda g: (g, 0, 0))
    return pl.pallas_call(
        functools.partial(local_kernel, tiles),
        grid=(lat_rows // GROUP,),
        in_specs=[
            pl.BlockSpec((GROUP, wide, chans), lambda g: (g, 0, 0)),
            pl.BlockSpec((1, wide, chans), lambda g: (g * GROUP + GROUP, 0, 0)),
            pl.BlockSpec((1, wide, chans), lambda g: (g * GROUP + GROUP + 1, 0, 0)),
            pl.BlockSpec((GROUP, basis_count, 256), lambda g: (g, 0, 0)),
            pl.BlockSpec(mixing.shape, lambda g: (0, 0, 0)),
            block,
        ],
        out_specs=block,
        out_shape=jax.ShapeDtypeStruct(fields.shape, jnp.bfloat16),
        scratch_shapes=[pltpu.VMEM((basis_count, GROUP * tiles * TILE, chans), jnp.bfloat16)],
        compiler_params=pltpu.CompilerParams(vmem_limit_bytes=LIMIT),
        cost_estimate=pl.CostEstimate(
            flops=2 * lat_rows * tiles * (256 * 256 * chans + TILE * basis_count * chans * chans),
            bytes_accessed=8 * padded.size,
            transcendentals=0,
        ),
        name="local",
    )(padded, padded, padded, taps, mixing, fields)


def add_kernel(base_ref, back_ref, o_ref):
    o_ref[...] = (base_ref[...].astype(jnp.float32) + back_ref[...].astype(jnp.float32)).astype(
        jnp.bfloat16
    )


def add_part(base, back, part):
    count, height, cols, chans = back.shape
    return pl.pallas_call(
        add_kernel,
        grid=(count,),
        in_specs=[
            pl.BlockSpec((1, height, cols, chans), lambda s: (s, part, 0, 0)),
            pl.BlockSpec((1, height, cols, chans), lambda s: (s, 0, 0, 0)),
        ],
        out_specs=pl.BlockSpec((1, height, cols, chans), lambda s: (s, part, 0, 0)),
        out_shape=jax.ShapeDtypeStruct(base.shape, jnp.bfloat16),
        input_output_aliases={0: 0},
        compiler_params=pltpu.CompilerParams(vmem_limit_bytes=LIMIT),
        cost_estimate=pl.CostEstimate(
            flops=back.size, bytes_accessed=6 * back.size, transcendentals=0
        ),
        name="add",
    )(base, back)


def shards(fields, basis, reach, mixing, gains):
    lat_rows, cols, chans = fields.shape
    count = lax.axis_size("lon")
    rows = lat_rows // count
    low, high = exchange(fields, "lon", 1, HALO, True)
    sent, low, high = lax.optimization_barrier((fields, low, high))
    split = sent.reshape(count, PARTS, rows // PARTS, cols, chans)
    gathered = [
        lax.all_to_all(split[:, q], "lon", split_axis=0, concat_axis=0, tiled=True)
        for q in range(PARTS)
    ]
    tiles = -(-cols // TILE)
    spare = jnp.zeros((lat_rows, tiles * TILE - cols, chans), jnp.bfloat16)
    wide = jnp.concatenate([low, fields, high, spare], 1)
    above, below = exchange(wide, "lat", 0, 1, False)
    padded = jnp.concatenate([above, wide, below], 0)
    offsets = jnp.arange(WIN, dtype=jnp.int32) - HALO
    mask = (jnp.abs(offsets)[None, :] <= reach[:, None]).astype(jnp.float32)
    filters = (basis * mask[:, None, None, :]).astype(jnp.bfloat16).astype(jnp.float32)
    taps = jnp.pad(filters, ((0, 0), (0, 0), (0, 0), (0, SPAN - WIN)))
    taps = jnp.pad(
        taps.reshape(lat_rows, basis.shape[1], 3 * SPAN), ((0, 0), (0, 0), (0, 256 - 3 * SPAN))
    )
    base = local_part(fields, padded, taps, mixing)
    forward, adjoint = tables(count, cols)
    first, base = lax.optimization_barrier((gathered[0], base))
    gathered = [first] + gathered[1:]
    backs = [
        lax.all_to_all(
            transform(piece, forward, adjoint, gains), "lon", split_axis=0, concat_axis=0, tiled=True
        )
        for piece in gathered
    ]
    total = base.reshape(count, rows, cols, chans)
    for part, back in enumerate(backs):
        total = add_part(total, back, part)
    return total.reshape(lat_rows, cols, chans)


def solution(mesh):
    return jax.shard_map(
        shards,
        mesh=mesh,
        in_specs=(P("lat", "lon", None), P("lat", None, None, None), P("lat"), P(), P()),
        out_specs=P("lat", "lon", None),
        check_vma=False,
    )
```

time: 1050 us -> 649 us (0.62)
  local copies, waits for them, and re-layouts: 265 us -> 91 us
  matrix products: 173 us -> 0 us
  waiting for transfers between devices: 499 us -> 348 us
  Pallas kernels: 0 us -> 110 us
  other arithmetic: 80.3 us -> 57.8 us
  starting transfers between devices: 22.8 us -> 35.2 us
    convert_element_type x4 -> x0, local copies, waits for them, and re-layouts: 235 us -> none  [the longest x1 175 us: shards(): band = jnp.einsum('ikab,jpb->ikjap', filters, select, preferred_element_t...]
    ppermute x4, waiting for transfers between devices: 260 us -> 26.7 us  [the longest x2 22.6 us: exchange(): lax.ppermute(lax.slice_in_dim(block, block.shape[dim] - width, None, axis...]
    dot_general x4 -> x0, matrix products: 173 us -> none  [the longest x1 81.1 us: shards(): jnp.einsum('ikjc,kcd->ijd', conv, mixing, preferred_element_type=jnp.floa...]
    pallas_call x0 -> x5, Pallas kernels: none -> 110 us  [the longest x2 53.8 us: transform(): pl.pallas_call(functools.partial(transform_kernel, count, cols, rows), gr...]
    all_to_all x2 -> x4, waiting for transfers between devices: 238 us -> 321 us  [the longest x2 199 us: shards(): lax.all_to_all(transform(piece, forward, adjoint, gains), 'lon', split_ax...]
    another operation x2 -> x0, other arithmetic: 46.1 us -> none  [the longest x1 32.2 us: shards(): jnp.stack([padded[0:lat_rows], padded[1:lat_rows + 1], padded[2:lat_rows...]
    cos x0 -> x1, other arithmetic: none -> 26.1 us  [tables(): forward = jnp.concatenate([jnp.cos(angle), -jnp.sin(angle)], 1)]
    neg x1 -> x0, other arithmetic: 19.7 us -> none  [make_tables(): forward = jnp.concatenate([cosine, -sine], 1)]
  transfers between devices with their start and end apart: 6 -> 8, of which waited for: 3 -> 5; matrix products, arithmetic and copies ran while one was open for 27% -> 17% of each run, Pallas kernels for 0% -> 16%
where the time goes in v1:
time: 649 us; the launch traced here: 642 us
  waiting for transfers between devices  348 us (54%)
  Pallas kernels  110 us (17%)
  local copies, waits for them, and re-layouts  91 us (14%)
  other arithmetic  57.8 us (9%)
  starting transfers between devices  35.2 us (5%)
    all_to_all x2, waiting for transfers between devices, shards(): lax.all_to_all(transform(piece, forward, adjoint, gains), 'lon', split_ax...  199 us
    all_to_all x2, waiting for transfers between devices, shards(): lax.all_to_all(split[:, q], 'lon', split_axis=0, concat_axis=0, tiled=True)  122 us
    pallas_call x2, Pallas kernels, transform(): pl.pallas_call(functools.partial(transform_kernel, count, cols, rows), gr...  53.8 us
    pallas_call x1, Pallas kernels, local_part(): pl.pallas_call(functools.partial(local_kernel, tiles), grid=(lat_rows //...  40.2 us
    cos x1, other arithmetic, tables(): forward = jnp.concatenate([jnp.cos(angle), -jnp.sin(angle)], 1)  26.1 us
    ppermute x2, waiting for transfers between devices, exchange(): lax.ppermute(lax.slice_in_dim(block, block.shape[dim] - width, None, axis...  22.6 us
    unnamed x20, local copies, waits for them, and re-layouts  22.3 us
    pallas_call x2, Pallas kernels, add_part(): pl.pallas_call(add_kernel, grid=(count,), in_specs=[pl.BlockSpec((1, heig...  16.5 us
  transfers between devices with their start and end apart: 8, of which 5 were waited for; matrix products, arithmetic and copies ran while one was open for 17% of the time, Pallas kernels for 16%

profile of v1, /device:TPU:13, one launch (start us, length us, event | category | flops | bytes accessed | tf_op | source)
XLA Modules:
  0.0 642.4 jit_solution(7742817730421367036)
XLA Ops:
  0.0 14.4 %copy.25.x_ref = bf16[128,180,256]{2,1,0:T(8,128)(2,1)} copy(bf16[128,180,256]{2,0,1:T(8,128)(2,1)} %param.5) | data formatting | bytes 23592960 | tf_op args[0]
  17.5 22.6 %collective-permute-done = bf16[128,8,256]{2,1,0:T(8,128)(2,1)S(1)} collective-permute-done((bf16[128,8,256]{2,1,0:T(8,128)(2,1)S(1)}, bf16[128,8,256]{2,1,0:T(8,128)(2,1)S(1)}, u32[]{:S(2)}, u32[]{:S(2)}) %collective-permute-start) | collective-permute-done | bytes 524320 | tf_op jit(solution)/shard_map/ppermute | solution.py:27
  40.1 3.1 slice_bitcast_fusion
  43.2 2.9 copy.27
  46.1 6.7 %all-to-all-start = ((bf16[8,8,180,256]{3,1,2,0:T(8,128)(2,1)}), bf16[8,8,180,256]{3,1,2,0:T(8,128)(2,1)}, u32[]{:S(2)}, u32[]{:S(2)}) async-start(bf16[8,8,180,256]{3,1,2,0:T(8,128)(2,1)} %copy.27), calls=%async_computation | async-start | bytes 11796480 | tf_op jit(solution)/shard_map/all_to_all | solution.py:200
  52.8 5.5 copy.36
  58.3 121.6 %all-to-all-done = bf16[8,8,180,256]{3,1,2,0:T(8,128)(2,1)} async-done(((bf16[8,8,180,256]{3,1,2,0:T(8,128)(2,1)}), bf16[8,8,180,256]{3,1,2,0:T(8,128)(2,1)}, u32[]{:S(2)}, u32[]{:S(2)}) %all-to-all-start) | async-done | bytes 5898272 | tf_op jit(solution)/shard_map/all_to_all | solution.py:200
  179.9 6.5 %all-to-all-start.2 = ((bf16[8,8,180,256]{3,1,2,0:T(8,128)(2,1)}), bf16[8,8,180,256]{3,1,2,0:T(8,128)(2,1)}, u32[]{:S(2)}, u32[]{:S(2)}) async-start(bf16[8,8,180,256]{3,1,2,0:T(8,128)(2,1)} %copy.36), calls=%async_computation.2 | async-start | bytes 11796480 | tf_op jit(solution)/shard_map/all_to_all | solution.py:200
  186.9 26.1 %fusion.6 = (f32[8,180,720]{1,2,0:T(8,128)}, f32[8,180,720]{1,2,0:T(8,128)}) fusion(s32[8,180]{1,0:T(8,128)S(1)} %multiply_add_fusion), kind=kLoop, calls=%fused_computation.14 | loop fusion | flops 10368000 | bytes 8300160 | tf_op jit(solution)/shard_map/cos | solution.py:43
  213.0 7.8 %multiply_convert_fusion = bf16[8,180,1440]{1,2,0:T(8,128)(2,1)} fusion(f32[8,180,720]{1,2,0:T(8,128)} %get-tuple-element.22, f32[8,180,720]{1,2,0:T(8,128)} %get-tuple-element.21, f32[1440]{0:T(1024)S(1)} %pad_maximum_fusion.6), kind=kLoop, calls=%fused_computation.2 | loop fusion | flops 6220800 | bytes 12447360 | tf_op jit(solution)/shard_map/convert_element_type | solution.py:46
  220.8 7.9 %copy.41 = bf16[8,180,1440]{2,1,0:T(8,128)(2,1)} copy(bf16[8,180,1440]{1,2,0:T(8,128)(2,1)} %multiply_convert_fusion) | data formatting | bytes 8294400
  228.7 4.8 pad.18.clone
  233.5 7.5 %fusion.3.f_ref = bf16[8,1440,180]{2,1,0:T(8,128)(2,1)} fusion(f32[8,180,720]{1,2,0:T(8,128)} %get-tuple-element.22, f32[8,180,720]{1,2,0:T(8,128)} %get-tuple-element.21), kind=kLoop, calls=%fused_computation.7 | loop fusion | flops 8294400 | bytes 12441600 | tf_op jit(solution)/shard_map/transpose | solution.py:50
  242.0 5.0 collective-permute-start.2
  249.3 4.2 collective-permute-done.3
  253.4 15.1 %pad_maximum_fusion.w_ref.n0_ref.n1_ref = bf16[130,208,256]{2,1,0:T(8,128)(2,1)} fusion(bf16[1,208,256]{2,1,0:T(8,128)(2,1)S(1)} %collective-permute-done.3, bf16[128,12,256]{2,1,0:T(8,128)(2,1)S(1)} %broadcast_in_dim.10, bf16[128,8,256]{2,1,0:T(8,128)(2,1)S(1)} %collective-permute-done.1, bf16[128,180,256]{2,1,0:T(8,128)(2,1)} %copy.25.x_ref, ...), kind=kLoop, calls=%fused_computation | loop fusion | flops 83066880 | bytes 27688960 | tf_op jit(solution)/shard_map/concatenate | solution.py:207
  268.6 40.2 %local.1 = bf16[128,180,256]{2,1,0:T(8,128)(2,1)} custom-call(bf16[130,208,256]{2,1,0:T(8,128)(2,1)} %pad_maximum_fusion.w_ref.n0_ref.n1_ref, bf16[130,208,256]{2,1,0:T(8,128)(2,1)} %pad_maximum_fusion.w_ref.n0_ref.n1_ref, bf16[130,208,256]{2,1,0:T(8,128)(2,1)} %pad_maximum_fusion.w_ref.n0_ref.n1_ref, f32[128,4,256]{2,1,0:T(4,128)S(1)} %pad_convert_fusion.taps_ref, ...), custom_call_target="tpu_custom_call" | custom-call | flops 25769803776 | bytes 55377920 | tf_op jit(solution)/shard_map/local/pallas_call | solution.py:142
  308.8 6.7 %copy.33.x_ref = bf16[8,8,180,256]{3,2,1,0:T(8,128)(2,1)} copy(bf16[8,8,180,256]{3,1,2,0:T(8,128)(2,1)} %all-to-all-done) | data formatting | bytes 11796480 | tf_op jit(solution)/shard_map/optimization_barrier | solution.py:217
  315.5 26.9 %transform.2 = bf16[8,8,180,256]{3,2,1,0:T(8,128)(2,1)} custom-call(bf16[8,8,180,256]{3,2,1,0:T(8,128)(2,1)} %copy.33.x_ref, bf16[8,1440,180]{2,1,0:T(8,128)(2,1)} %fusion.3.f_ref, bf16[1472,1440]{1,0:T(8,128)(2,1)S(1)} %bitcast.13, f32[2,720,256]{2,1,0:T(8,128)S(1)} %copy-done), custom_call_target="tpu_custom_call" | custom-call | flops 16986931200 | bytes 23796480 | tf_op jit(solution)/shard_map/transform/pallas_call | solution.py:79
  342.4 6.5 %copy.34 = bf16[8,8,180,256]{3,1,2,0:T(8,128)(2,1)} copy(bf16[8,8,180,256]{3,2,1,0:T(8,128)(2,1)} %transform.2) | data formatting | bytes 11796480 | tf_op jit(solution)/shard_map/transform/pallas_call | solution.py:79
  348.9 5.6 all-to-all-start.1
  354.5 6.7 %copy.37.x_ref = bf16[8,8,180,256]{3,2,1,0:T(8,128)(2,1)} copy(bf16[8,8,180,256]{3,1,2,0:T(8,128)(2,1)} %all-to-all-done.2) | data formatting | bytes 11796480 | tf_op jit(solution)/shard_map/all_to_all | solution.py:200
  361.2 26.9 %transform.3 = bf16[8,8,180,256]{3,2,1,0:T(8,128)(2,1)} custom-call(bf16[8,8,180,256]{3,2,1,0:T(8,128)(2,1)} %copy.37.x_ref, bf16[8,1440,180]{2,1,0:T(8,128)(2,1)} %fusion.3.f_ref, bf16[1472,1440]{1,0:T(8,128)(2,1)S(1)} %bitcast.16, f32[2,720,256]{2,1,0:T(8,128)S(1)} %copy-done), custom_call_target="tpu_custom_call" | custom-call | flops 16986931200 | bytes 23796480 | tf_op jit(solution)/shard_map/transform/pallas_call | solution.py:79
  388.1 6.5 %copy.38 = bf16[8,8,180,256]{3,1,2,0:T(8,128)(2,1)} copy(bf16[8,8,180,256]{3,2,1,0:T(8,128)(2,1)} %transform.3) | data formatting | bytes 11796480 | tf_op jit(solution)/shard_map/transform/pallas_call | solution.py:79
  394.6 84.7 %all-to-all-done.1 = bf16[8,8,180,256]{3,1,2,0:T(8,128)(2,1)} async-done(((bf16[8,8,180,256]{3,1,2,0:T(8,128)(2,1)}), bf16[8,8,180,256]{3,1,2,0:T(8,128)(2,1)}, u32[]{:S(2)}, u32[]{:S(2)}) %all-to-all-start.1) | async-done | bytes 5898272 | tf_op jit(solution)/shard_map/all_to_all | solution.py:220
  479.3 7.8 %all-to-all-start.3 = ((bf16[8,8,180,256]{3,1,2,0:T(8,128)(2,1)}), bf16[8,8,180,256]{3,1,2,0:T(8,128)(2,1)}, u32[]{:S(2)}, u32[]{:S(2)}) async-start(bf16[8,8,180,256]{3,1,2,0:T(8,128)(2,1)} %copy.38), calls=%async_computation.3 | async-start | bytes 11796480 | tf_op jit(solution)/shard_map/all_to_all | solution.py:220
  487.1 3.9 copy.35.back_ref
  491.0 8.2 %add.38.base_ref = bf16[8,16,180,256]{3,2,1,0:T(8,128)(2,1)} custom-call(bf16[8,16,180,256]{3,2,1,0:T(8,128)(2,1)} %bitcast.17, bf16[8,8,180,256]{3,2,1,0:T(8,128)(2,1)S(1)} %copy.35.back_ref), custom_call_target="tpu_custom_call", output_to_operand_aliasing={{}: (0, {})} | custom-call | flops 2949120 | bytes 17694720 | tf_op jit(solution)/shard_map/add/pallas_call | solution.py:174
  499.3 114.8 %all-to-all-done.3 = bf16[8,8,180,256]{3,1,2,0:T(8,128)(2,1)} async-done(((bf16[8,8,180,256]{3,1,2,0:T(8,128)(2,1)}), bf16[8,8,180,256]{3,1,2,0:T(8,128)(2,1)}, u32[]{:S(2)}, u32[]{:S(2)}) %all-to-all-start.3) | async-done | bytes 5898272 | tf_op jit(solution)/shard_map/all_to_all | solution.py:220
  614.0 3.9 copy.39.back_ref
  618.0 8.2 %add.39 = bf16[8,16,180,256]{3,2,1,0:T(8,128)(2,1)} custom-call(bf16[8,16,180,256]{3,2,1,0:T(8,128)(2,1)} %add.38.base_ref, bf16[8,8,180,256]{3,2,1,0:T(8,128)(2,1)S(1)} %copy.39.back_ref), custom_call_target="tpu_custom_call", output_to_operand_aliasing={{}: (0, {})} | custom-call | flops 2949120 | bytes 17694720 | tf_op jit(solution)/shard_map/add/pallas_call | solution.py:174
  626.2 16.1 %copy.40 = bf16[128,180,256]{2,0,1:T(8,128)(2,1)} copy(bf16[128,180,256]{2,1,0:T(8,128)(2,1)} %bitcast.18) | data formatting | bytes 23592960 | tf_op jit(solution)/shard_map/reshape | solution.py:228
  (38 shorter events, 6.8 us)
Async XLA Ops:
  0.0 40.1 %copy-start.2 = (bf16[128,180,256]{2,0,1:T(8,128)(2,1)S(1)}, bf16[128,180,256]{2,0,1:T(8,128)(2,1)}, u32[]{:S(2)}) copy-start(bf16[128,180,256]{2,0,1:T(8,128)(2,1)} %param.5) | copy-start | bytes 35389444
  16.0 24.1 %collective-permute-start = (bf16[128,8,256]{2,1,0:T(8,128)(2,1)S(1)}, bf16[128,8,256]{2,1,0:T(8,128)(2,1)S(1)}, u32[]{:S(2)}, u32[]{:S(2)}) collective-permute-start(bf16[128,8,256]{2,1,0:T(8,128)(2,1)S(1)} %get-tuple-element.18), channel_id=1, source_target_pairs={{0,1},{1,2},{2,3},{3,4},{4,5},{5,6},{6,7},{7,0},{8,9},{9,10},{10,1... | collective-permute-start | bytes 1572872 | tf_op jit(solution)/shard_map/ppermute | solution.py:27
  17.3 22.8 %collective-permute-start.1 = (bf16[128,8,256]{2,1,0:T(8,128)(2,1)S(1)}, bf16[128,8,256]{2,1,0:T(8,128)(2,1)S(1)}, u32[]{:S(2)}, u32[]{:S(2)}) collective-permute-start(bf16[128,8,256]{2,1,0:T(8,128)(2,1)S(1)} %get-tuple-element.17), channel_id=1, source_target_pairs={{1,0},{2,1},{3,2},{4,3},{5,4},{6,5},{7,6},{0,7},{9,8},{10,9},{11,1... | collective-permute-start | bytes 1572872 | tf_op jit(solution)/shard_map/ppermute | solution.py:30
  46.1 133.8 %all-to-all-start = ((bf16[8,8,180,256]{3,1,2,0:T(8,128)(2,1)}), bf16[8,8,180,256]{3,1,2,0:T(8,128)(2,1)}, u32[]{:S(2)}, u32[]{:S(2)}) async-start(bf16[8,8,180,256]{3,1,2,0:T(8,128)(2,1)} %copy.27), calls=%async_computation | async-start | bytes 11796480 | tf_op jit(solution)/shard_map/all_to_all | solution.py:200
  58.3 128.2 %copy-start.4 = (s32[128]{0:T(128)S(1)}, s32[128]{0:T(128)}, u32[]{:S(2)}) copy-start(s32[128]{0:T(128)} %param.7) | copy-start | bytes 1540
  58.3 128.2 %copy-start.3 = (f32[128,4,3,17]{0,1,3,2:T(4,128)S(1)}, f32[128,4,3,17]{0,1,3,2:T(4,128)}, u32[]{:S(2)}) copy-start(f32[128,4,3,17]{0,1,3,2:T(4,128)} %param.6) | copy-start | bytes 313348
  179.9 169.0 %all-to-all-start.2 = ((bf16[8,8,180,256]{3,1,2,0:T(8,128)(2,1)}), bf16[8,8,180,256]{3,1,2,0:T(8,128)(2,1)}, u32[]{:S(2)}, u32[]{:S(2)}) async-start(bf16[8,8,180,256]{3,1,2,0:T(8,128)(2,1)} %copy.36), calls=%async_computation.2 | async-start | bytes 11796480 | tf_op jit(solution)/shard_map/all_to_all | solution.py:200
  242.0 7.3 %collective-permute-start.2 = (bf16[1,208,256]{2,1,0:T(8,128)(2,1)S(1)}, bf16[1,208,256]{2,1,0:T(8,128)(2,1)S(1)}, u32[]{:S(2)}, u32[]{:S(2)}) collective-permute-start(bf16[1,208,256]{2,1,0:T(8,128)(2,1)S(1)} %get-tuple-element.15), channel_id=1, source_target_pairs={{0,8},{8,16},{16,24},{1,9},{9,17},{17,25},{2,10},{10,18},{18,26},{... | collective-permute-start | bytes 319496 | tf_op jit(solution)/shard_map/ppermute | solution.py:27
  247.0 6.4 collective-permute-start.3
  249.2 19.3 %copy-start.1 = (bf16[4,256,256]{2,1,0:T(8,128)(2,1)S(1)}, bf16[4,256,256]{2,1,0:T(8,128)(2,1)}, u32[]{:S(2)}) copy-start(bf16[4,256,256]{2,1,0:T(8,128)(2,1)} %mix_ref.1) | copy-start | bytes 1572868
  253.4 62.1 %slice-start = ((s8[4521984]{0:T(1024)(128)(4,1)}), s8[4194304]{0:T(1024)(128)(4,1)S(1)}, s32[]{:S(2)}) async-start(s8[4521984]{0:T(1024)(128)(4,1)} %bitcast.11), calls=%async_computation.4 | async-start | bytes 8388608
  268.6 46.9 %slice-start.1 = ((s8[4521984]{0:T(1024)(128)(4,1)}), s8[327680]{0:T(1024)(128)(4,1)S(1)}, s32[]{:S(2)}) async-start(s8[4521984]{0:T(1024)(128)(4,1)} %bitcast.11), calls=%async_computation.5 | async-start | bytes 655360
  308.8 6.7 %copy-start = (f32[2,720,256]{2,1,0:T(8,128)S(1)}, f32[2,720,256]{2,1,0:T(8,128)}, u32[]{:S(2)}) copy-start(f32[2,720,256]{2,1,0:T(8,128)} %g_ref.3) | copy-start | bytes 4423684
  348.9 12.3 %slice-start.2 = ((s8[4521984]{0:T(1024)(128)(4,1)}), s8[327680]{0:T(1024)(128)(4,1)S(1)}, s32[]{:S(2)}) async-start(s8[4521984]{0:T(1024)(128)(4,1)} %bitcast.14), calls=%async_computation.6 | async-start | bytes 655360
  348.9 130.4 %all-to-all-start.1 = ((bf16[8,8,180,256]{3,1,2,0:T(8,128)(2,1)}), bf16[8,8,180,256]{3,1,2,0:T(8,128)(2,1)}, u32[]{:S(2)}, u32[]{:S(2)}) async-start(bf16[8,8,180,256]{3,1,2,0:T(8,128)(2,1)} %copy.34), calls=%async_computation.1 | async-start | bytes 11796480 | tf_op jit(solution)/shard_map/all_to_all | solution.py:220
  354.5 6.7 %slice-start.3 = ((s8[4521984]{0:T(1024)(128)(4,1)}), s8[4194304]{0:T(1024)(128)(4,1)S(1)}, s32[]{:S(2)}) async-start(s8[4521984]{0:T(1024)(128)(4,1)} %bitcast.14), calls=%async_computation.7 | async-start | bytes 8388608
  479.3 134.8 %all-to-all-start.3 = ((bf16[8,8,180,256]{3,1,2,0:T(8,128)(2,1)}), bf16[8,8,180,256]{3,1,2,0:T(8,128)(2,1)}, u32[]{:S(2)}, u32[]{:S(2)}) async-start(bf16[8,8,180,256]{3,1,2,0:T(8,128)(2,1)} %copy.38), calls=%async_computation.3 | async-start | bytes 11796480 | tf_op jit(solution)/shard_map/all_to_all | solution.py:220

commit v2 on v1

--- a/solution.py
+++ b/solution.py
@@ -164,21 +164,24 @@
 
 
 def add_kernel(base_ref, back_ref, o_ref):
-    o_ref[...] = (base_ref[...].astype(jnp.float32) + back_ref[...].astype(jnp.float32)).astype(
-        jnp.bfloat16
-    )
+    for s in range(back_ref.shape[0]):
+        o_ref[:, s, 0] = (
+            base_ref[:, s, 0].astype(jnp.float32) + back_ref[s].astype(jnp.float32)
+        ).astype(jnp.bfloat16)
 
 
 def add_part(base, back, part):
-    count, height, cols, chans = back.shape
+    count, cols, height, chans = back.shape
+    steps = 9 if cols % 9 == 0 else 1
+    wide = pl.BlockSpec((cols // steps, count, 1, height, chans), lambda j: (j, 0, part, 0, 0))
     return pl.pallas_call(
         add_kernel,
-        grid=(count,),
+        grid=(steps,),
         in_specs=[
-            pl.BlockSpec((1, height, cols, chans), lambda s: (s, part, 0, 0)),
-            pl.BlockSpec((1, height, cols, chans), lambda s: (s, 0, 0, 0)),
+            wide,
+            pl.BlockSpec((count, cols // steps, height, chans), lambda j: (0, j, 0, 0)),
         ],
-        out_specs=pl.BlockSpec((1, height, cols, chans), lambda s: (s, part, 0, 0)),
+        out_specs=wide,
         out_shape=jax.ShapeDtypeStruct(base.shape, jnp.bfloat16),
         input_output_aliases={0: 0},
         compiler_params=pltpu.CompilerParams(vmem_limit_bytes=LIMIT),
@@ -193,13 +196,18 @@
     lat_rows, cols, chans = fields.shape
     count = lax.axis_size("lon")
     rows = lat_rows // count
-    low, high = exchange(fields, "lon", 1, HALO, True)
-    sent, low, high = lax.optimization_barrier((fields, low, high))
-    split = sent.reshape(count, PARTS, rows // PARTS, cols, chans)
-    gathered = [
-        lax.all_to_all(split[:, q], "lon", split_axis=0, concat_axis=0, tiled=True)
-        for q in range(PARTS)
-    ]
+    split = fields.reshape(count, PARTS, rows // PARTS, cols, chans)
+
+    def swap(piece):
+        return lax.all_to_all(piece, "lon", split_axis=0, concat_axis=0, tiled=True)
+
+    gathered = [swap(split[:, q]) for q in range(PARTS)]
+    first, forward, adjoint = lax.optimization_barrier((gathered[0], *tables(count, cols)))
+    results = [transform(piece, forward, adjoint, gains) for piece in [first] + gathered[1:]]
+    near, _ = lax.optimization_barrier((fields, first))
+    low, high = exchange(near, "lon", 1, HALO, True)
+    ready, low, high = lax.optimization_barrier((results[0], low, high))
+    backs = [swap(ready)]
     tiles = -(-cols // TILE)
     spare = jnp.zeros((lat_rows, tiles * TILE - cols, chans), jnp.bfloat16)
     wide = jnp.concatenate([low, fields, high, spare], 1)
@@ -213,19 +221,12 @@
         taps.reshape(lat_rows, basis.shape[1], 3 * SPAN), ((0, 0), (0, 0), (0, 256 - 3 * SPAN))
     )
     base = local_part(fields, padded, taps, mixing)
-    forward, adjoint = tables(count, cols)
-    first, base = lax.optimization_barrier((gathered[0], base))
-    gathered = [first] + gathered[1:]
-    backs = [
-        lax.all_to_all(
-            transform(piece, forward, adjoint, gains), "lon", split_axis=0, concat_axis=0, tiled=True
-        )
-        for piece in gathered
-    ]
-    total = base.reshape(count, rows, cols, chans)
+    *ready, base = lax.optimization_barrier((*results[1:], base))
+    backs += [swap(result) for result in ready]
+    total = base.transpose(1, 0, 2).reshape(cols, count, PARTS, rows // PARTS, chans)
     for part, back in enumerate(backs):
-        total = add_part(total, back, part)
-    return total.reshape(lat_rows, cols, chans)
+        total = add_part(total, back.transpose(0, 2, 1, 3), part)
+    return total.reshape(cols, lat_rows, chans).transpose(1, 0, 2)
 
 
 def solution(mesh):

time: 649 us -> 580 us (0.89)
  waiting for transfers between devices: 348 us -> 270 us
    all_to_all x4, waiting for transfers between devices: 321 us -> 235 us  [swap(): return lax.all_to_all(piece, 'lon', split_axis=0, concat_axis=0, tiled=True)]
    ppermute x2, waiting for transfers between devices: 4.16 us -> 35.5 us  [exchange(): lax.ppermute(lax.slice_in_dim(block, 0, width, axis=dim), axis, backward)]
    optimization_barrier x1 -> x4, local copies, waits for them, and re-layouts: 6.67 us -> 29 us  [the longest x1 12.1 us: shards(): near, _ = lax.optimization_barrier((fields, first))]
    ppermute x2, waiting for transfers between devices: 22.6 us -> 0.24 us  [exchange(): lax.ppermute(lax.slice_in_dim(block, block.shape[dim] - width, None, axis...]
    reshape x1 -> x0, local copies, waits for them, and re-layouts: 16.1 us -> none  [shards(): return total.reshape(lat_rows, cols, chans)]
    transpose x0 -> x1, local copies, waits for them, and re-layouts: none -> 16.1 us  [shards(): base.transpose(1, 0, 2).reshape(cols, count, PARTS, rows // PARTS, chans)]
    pallas_call x2 -> x0, local copies, waits for them, and re-layouts: 13 us -> none  [transform(): pl.pallas_call(functools.partial(transform_kernel, count, cols, rows), gr...]
    all_to_all x3 -> x1, local copies, waits for them, and re-layouts: 14.6 us -> 6.72 us  [swap(): return lax.all_to_all(piece, 'lon', split_axis=0, concat_axis=0, tiled=True)]
  transfers between devices with their start and end apart: 8 -> 8, of which waited for: 5 -> 5; matrix products, arithmetic and copies ran while one was open for 17% -> 25% of each run, Pallas kernels for 16% -> 18%
where the time goes in v2:
time: 580 us; the launch traced here: 573 us
  waiting for transfers between devices  270 us (47%)
  Pallas kernels  114 us (20%)
  local copies, waits for them, and re-layouts  95.3 us (16%)
  other arithmetic  58 us (10%)
  starting transfers between devices  35.2 us (6%)
    all_to_all x4, waiting for transfers between devices, swap(): return lax.all_to_all(piece, 'lon', split_axis=0, concat_axis=0, tiled=True)  235 us
    pallas_call x2, Pallas kernels, transform(): pl.pallas_call(functools.partial(transform_kernel, count, cols, rows), gr...  53.7 us
    pallas_call x1, Pallas kernels, local_part(): pl.pallas_call(functools.partial(local_kernel, tiles), grid=(lat_rows //...  40.3 us
    ppermute x2, waiting for transfers between devices, exchange(): lax.ppermute(lax.slice_in_dim(block, 0, width, axis=dim), axis, backward)  35.5 us
    cos x1, other arithmetic, tables(): forward = jnp.concatenate([jnp.cos(angle), -jnp.sin(angle)], 1)  26.1 us
    all_to_all x4, starting transfers between devices, swap(): return lax.all_to_all(piece, 'lon', split_axis=0, concat_axis=0, tiled=True)  26.1 us
    unnamed x22, local copies, waits for them, and re-layouts  21.7 us
    pallas_call x2, Pallas kernels, add_part(): pl.pallas_call(add_kernel, grid=(steps,), in_specs=[wide, pl.BlockSpec((c...  20.4 us
  transfers between devices with their start and end apart: 8, of which 5 were waited for; matrix products, arithmetic and copies ran while one was open for 25% of the time, Pallas kernels for 18%

profile of v2, /device:TPU:13, one launch (start us, length us, event | category | flops | bytes accessed | tf_op | source)
XLA Modules:
  0.0 573.4 jit_solution(14060224094849787936)
XLA Ops:
  0.0 7.9 %slice_bitcast_fusion = (bf16[8,8,180,256]{3,1,0,2:T(8,128)(2,1)S(1)}, bf16[8,8,180,256]{3,1,0,2:T(8,128)(2,1)}) fusion(bf16[8,2,8,180,256]{4,2,1,0,3:T(8,128)(2,1)} %bitcast.23), kind=kLoop, calls=%fused_computation.8 | loop fusion | bytes 23592960 | tf_op jit(solution)/shard_map/squeeze | solution.py:204
  7.9 2.9 copy.30
  10.9 5.7 all-to-all-start.1
  16.5 5.6 copy.29
  22.1 121.6 %all-to-all-done.1 = bf16[8,8,180,256]{3,1,2,0:T(8,128)(2,1)} async-done(((bf16[8,8,180,256]{3,1,2,0:T(8,128)(2,1)}), bf16[8,8,180,256]{3,1,2,0:T(8,128)(2,1)}, u32[]{:S(2)}, u32[]{:S(2)}) %all-to-all-start.1) | async-done | bytes 5898272 | tf_op jit(solution)/shard_map/all_to_all | solution.py:202
  143.7 6.5 %all-to-all-start = ((bf16[8,8,180,256]{3,1,2,0:T(8,128)(2,1)}), bf16[8,8,180,256]{3,1,2,0:T(8,128)(2,1)}, u32[]{:S(2)}, u32[]{:S(2)}) async-start(bf16[8,8,180,256]{3,1,2,0:T(8,128)(2,1)} %copy.29), calls=%async_computation | async-start | bytes 11796480 | tf_op jit(solution)/shard_map/all_to_all | solution.py:202
  150.2 26.1 %fusion.6 = (f32[8,180,720]{1,2,0:T(8,128)}, f32[8,180,720]{1,2,0:T(8,128)}) fusion(s32[8,180]{1,0:T(8,128)S(1)} %multiply_add_fusion), kind=kLoop, calls=%fused_computation.14 | loop fusion | flops 10368000 | bytes 8300160 | tf_op jit(solution)/shard_map/cos | solution.py:43
  176.4 7.8 %multiply_convert_fusion = bf16[8,180,1440]{1,2,0:T(8,128)(2,1)} fusion(f32[8,180,720]{1,2,0:T(8,128)} %get-tuple-element.30, f32[8,180,720]{1,2,0:T(8,128)} %get-tuple-element.29, f32[1440]{0:T(1024)S(1)} %pad_maximum_fusion.6), kind=kLoop, calls=%fused_computation.2 | loop fusion | flops 6220800 | bytes 12447360 | tf_op jit(solution)/shard_map/convert_element_type | solution.py:46
  184.2 7.8 %copy.43 = bf16[8,180,1440]{2,1,0:T(8,128)(2,1)} copy(bf16[8,180,1440]{1,2,0:T(8,128)(2,1)} %multiply_convert_fusion) | data formatting | bytes 8294400
  192.0 4.8 pad.15.clone
  196.8 7.6 %fusion.3.f_ref = bf16[8,1440,180]{2,1,0:T(8,128)(2,1)} fusion(f32[8,180,720]{1,2,0:T(8,128)} %get-tuple-element.30, f32[8,180,720]{1,2,0:T(8,128)} %get-tuple-element.29), kind=kLoop, calls=%fused_computation.7 | loop fusion | flops 8294400 | bytes 12441600 | tf_op jit(solution)/shard_map/transpose | solution.py:50
  204.4 6.7 %copy.33.x_ref = bf16[8,8,180,256]{3,2,1,0:T(8,128)(2,1)} copy(bf16[8,8,180,256]{3,1,2,0:T(8,128)(2,1)} %all-to-all-done.1) | data formatting | bytes 11796480 | tf_op jit(solution)/shard_map/optimization_barrier | solution.py:205
  211.1 12.1 %copy.34 = bf16[128,180,256]{2,1,0:T(8,128)(2,1)S(1)} copy(bf16[128,180,256]{2,0,1:T(8,128)(2,1)} %param.5) | data formatting | bytes 23592960 | tf_op jit(solution)/shard_map/optimization_barrier | solution.py:207
  223.7 2.1 collective-permute-start
  225.8 26.9 %transform.3 = bf16[8,8,180,256]{3,2,1,0:T(8,128)(2,1)} custom-call(bf16[8,8,180,256]{3,2,1,0:T(8,128)(2,1)} %copy.33.x_ref, bf16[8,1440,180]{2,1,0:T(8,128)(2,1)} %fusion.3.f_ref, bf16[1472,1440]{1,0:T(8,128)(2,1)S(1)} %bitcast.18, f32[2,720,256]{2,1,0:T(8,128)S(1)} %copy-done), custom_call_target="tpu_custom_call" | custom-call | flops 16986931200 | bytes 23796480 | tf_op jit(solution)/shard_map/transform/pallas_call | solution.py:79
  252.7 35.5 %collective-permute-done.1 = bf16[128,8,256]{2,1,0:T(8,128)(2,1)S(1)} collective-permute-done((bf16[128,8,256]{2,1,0:T(8,128)(2,1)S(1)}, bf16[128,8,256]{2,1,0:T(8,128)(2,1)S(1)}, u32[]{:S(2)}, u32[]{:S(2)}) %collective-permute-start.1) | collective-permute-done | bytes 524320 | tf_op jit(solution)/shard_map/ppermute | solution.py:30
  288.4 6.4 %copy.41 = bf16[8,8,180,256]{3,1,2,0:T(8,128)(2,1)} copy(bf16[8,8,180,256]{3,2,1,0:T(8,128)(2,1)} %transform.3) | data formatting | bytes 11796480 | tf_op jit(solution)/shard_map/optimization_barrier | solution.py:209
  294.9 5.6 all-to-all-start.2
  300.4 13.8 %copy.36.x_ref = bf16[128,180,256]{2,1,0:T(8,128)(2,1)} copy(bf16[128,180,256]{2,0,1:T(8,128)(2,1)} %param.5) | data formatting | bytes 23592960 | tf_op args[0]
  314.8 6.7 %copy.32.x_ref = bf16[8,8,180,256]{3,2,1,0:T(8,128)(2,1)} copy(bf16[8,8,180,256]{3,1,2,0:T(8,128)(2,1)} %all-to-all-done) | data formatting | bytes 11796480 | tf_op jit(solution)/shard_map/all_to_all | solution.py:202
  322.6 4.6 collective-permute-start.2
  327.1 2.1 collective-permute-start.3
  329.3 26.8 %transform.2 = bf16[8,8,180,256]{3,2,1,0:T(8,128)(2,1)} custom-call(bf16[8,8,180,256]{3,2,1,0:T(8,128)(2,1)} %copy.32.x_ref, bf16[8,1440,180]{2,1,0:T(8,128)(2,1)} %fusion.3.f_ref, bf16[1472,1440]{1,0:T(8,128)(2,1)S(1)} %bitcast.21, f32[2,720,256]{2,1,0:T(8,128)S(1)} %copy-done), custom_call_target="tpu_custom_call" | custom-call | flops 16986931200 | bytes 23796480 | tf_op jit(solution)/shard_map/transform/pallas_call | solution.py:79
  356.2 15.2 %pad_maximum_fusion.w_ref.n0_ref.n1_ref = bf16[130,208,256]{2,1,0:T(8,128)(2,1)} fusion(bf16[1,208,256]{2,1,0:T(8,128)(2,1)S(1)} %collective-permute-done.3, bf16[128,12,256]{2,1,0:T(8,128)(2,1)S(1)} %broadcast_in_dim.19, bf16[128,8,256]{2,1,0:T(8,128)(2,1)S(1)} %collective-permute-done.1, bf16[128,180,256]{2,1,0:T(8,128)(2,1)} %copy.36.x_ref, ...), kind=kLoop, calls=%fused_computation | loop fusion | flops 83066880 | bytes 27688960 | tf_op jit(solution)/shard_map/concatenate | solution.py:215
  371.4 40.3 %local.1 = bf16[128,180,256]{2,1,0:T(8,128)(2,1)} custom-call(bf16[130,208,256]{2,1,0:T(8,128)(2,1)} %pad_maximum_fusion.w_ref.n0_ref.n1_ref, bf16[130,208,256]{2,1,0:T(8,128)(2,1)} %pad_maximum_fusion.w_ref.n0_ref.n1_ref, bf16[130,208,256]{2,1,0:T(8,128)(2,1)} %pad_maximum_fusion.w_ref.n0_ref.n1_ref, f32[128,4,256]{2,1,0:T(4,128)S(1)} %pad_convert_fusion.taps_ref, ...), custom_call_target="tpu_custom_call" | custom-call | flops 25769803776 | bytes 55377920 | tf_op jit(solution)/shard_map/local/pallas_call | solution.py:142
  411.7 3.8 copy.42
  415.5 12.1 %all-to-all-done.2 = bf16[8,8,180,256]{3,1,2,0:T(8,128)(2,1)} async-done(((bf16[8,8,180,256]{3,1,2,0:T(8,128)(2,1)}), bf16[8,8,180,256]{3,1,2,0:T(8,128)(2,1)}, u32[]{:S(2)}, u32[]{:S(2)}) %all-to-all-start.2) | async-done | bytes 5898272 | tf_op jit(solution)/shard_map/all_to_all | solution.py:202
  427.6 8.4 %all-to-all-start.3 = ((bf16[8,8,180,256]{3,1,2,0:T(8,128)(2,1)}), bf16[8,8,180,256]{3,1,2,0:T(8,128)(2,1)}, u32[]{:S(2)}, u32[]{:S(2)}) async-start(bf16[8,8,180,256]{3,1,2,0:T(8,128)(2,1)} %copy.42), calls=%async_computation.3 | async-start | bytes 11796480 | tf_op jit(solution)/shard_map/all_to_all | solution.py:202
  436.1 16.1 %copy.40 = bf16[180,128,256]{2,1,0:T(8,128)(2,1)} copy(bf16[180,128,256]{2,0,1:T(8,128)(2,1)} %bitcast.24) | data formatting | bytes 23592960 | tf_op jit(solution)/shard_map/transpose | solution.py:226
  452.2 10.2 %add.38.base_ref = bf16[180,8,2,8,256]{4,3,2,1,0:T(8,128)(2,1)} custom-call(bf16[180,8,2,8,256]{4,3,2,1,0:T(8,128)(2,1)} %bitcast.22, bf16[8,180,8,256]{3,2,1,0:T(8,128)(2,1)} %bitcast.8.back_ref), custom_call_target="tpu_custom_call", output_to_operand_aliasing={{}: (0, {})} | custom-call | flops 2949120 | bytes 17694720 | tf_op jit(solution)/shard_map/add/pallas_call | solution.py:177
  462.4 100.8 %all-to-all-done.3 = bf16[8,8,180,256]{3,1,2,0:T(8,128)(2,1)} async-done(((bf16[8,8,180,256]{3,1,2,0:T(8,128)(2,1)}), bf16[8,8,180,256]{3,1,2,0:T(8,128)(2,1)}, u32[]{:S(2)}, u32[]{:S(2)}) %all-to-all-start.3) | async-done | bytes 5898272 | tf_op jit(solution)/shard_map/all_to_all | solution.py:202
  563.2 10.2 %add.39 = bf16[180,8,2,8,256]{4,3,2,1,0:T(8,128)(2,1)} custom-call(bf16[180,8,2,8,256]{4,3,2,1,0:T(8,128)(2,1)} %add.38.base_ref, bf16[8,180,8,256]{3,2,1,0:T(8,128)(2,1)} %bitcast.9.back_ref), custom_call_target="tpu_custom_call", output_to_operand_aliasing={{}: (0, {})} | custom-call | flops 2949120 | bytes 17694720 | tf_op jit(solution)/shard_map/add/pallas_call | solution.py:177
  (40 shorter events, 2.4 us)
Async XLA Ops:
  10.9 132.8 %all-to-all-start.1 = ((bf16[8,8,180,256]{3,1,2,0:T(8,128)(2,1)}), bf16[8,8,180,256]{3,1,2,0:T(8,128)(2,1)}, u32[]{:S(2)}, u32[]{:S(2)}) async-start(bf16[8,8,180,256]{3,1,2,0:T(8,128)(2,1)} %copy.30), calls=%async_computation.1 | async-start | bytes 11796480 | tf_op jit(solution)/shard_map/all_to_all | solution.py:202
  143.7 151.2 %all-to-all-start = ((bf16[8,8,180,256]{3,1,2,0:T(8,128)(2,1)}), bf16[8,8,180,256]{3,1,2,0:T(8,128)(2,1)}, u32[]{:S(2)}, u32[]{:S(2)}) async-start(bf16[8,8,180,256]{3,1,2,0:T(8,128)(2,1)} %copy.29), calls=%async_computation | async-start | bytes 11796480 | tf_op jit(solution)/shard_map/all_to_all | solution.py:202
  204.4 21.4 %slice-start = ((s8[4521984]{0:T(1024)(128)(4,1)}), s8[4194304]{0:T(1024)(128)(4,1)S(1)}, s32[]{:S(2)}) async-start(s8[4521984]{0:T(1024)(128)(4,1)} %bitcast.16), calls=%async_computation.4 | async-start | bytes 8388608
  211.1 14.7 %slice-start.1 = ((s8[4521984]{0:T(1024)(128)(4,1)}), s8[327680]{0:T(1024)(128)(4,1)S(1)}, s32[]{:S(2)}) async-start(s8[4521984]{0:T(1024)(128)(4,1)} %bitcast.16), calls=%async_computation.5 | async-start | bytes 655360
  211.1 14.7 %copy-start = (f32[2,720,256]{2,1,0:T(8,128)S(1)}, f32[2,720,256]{2,1,0:T(8,128)}, u32[]{:S(2)}) copy-start(f32[2,720,256]{2,1,0:T(8,128)} %g_ref.3) | copy-start | bytes 4423684
  223.4 64.8 %collective-permute-start.1 = (bf16[128,8,256]{2,1,0:T(8,128)(2,1)S(1)}, bf16[128,8,256]{2,1,0:T(8,128)(2,1)S(1)}, u32[]{:S(2)}, u32[]{:S(2)}) collective-permute-start(bf16[128,8,256]{2,1,0:T(8,128)(2,1)S(1)} %get-tuple-element.25), channel_id=1, source_target_pairs={{1,0},{2,1},{3,2},{4,3},{5,4},{6,5},{7,6},{0,7},{9,8},{10,9},{11,1... | collective-permute-start | bytes 1572872 | tf_op jit(solution)/shard_map/ppermute | solution.py:30
  223.7 64.7 %collective-permute-start = (bf16[128,8,256]{2,1,0:T(8,128)(2,1)S(1)}, bf16[128,8,256]{2,1,0:T(8,128)(2,1)S(1)}, u32[]{:S(2)}, u32[]{:S(2)}) collective-permute-start(bf16[128,8,256]{2,1,0:T(8,128)(2,1)S(1)} %get-tuple-element.26), channel_id=1, source_target_pairs={{0,1},{1,2},{2,3},{3,4},{4,5},{5,6},{6,7},{7,0},{8,9},{9,10},{10,1... | collective-permute-start | bytes 1572872 | tf_op jit(solution)/shard_map/ppermute | solution.py:27
  294.9 132.7 %all-to-all-start.2 = ((bf16[8,8,180,256]{3,1,2,0:T(8,128)(2,1)}), bf16[8,8,180,256]{3,1,2,0:T(8,128)(2,1)}, u32[]{:S(2)}, u32[]{:S(2)}) async-start(bf16[8,8,180,256]{3,1,2,0:T(8,128)(2,1)} %copy.41), calls=%async_computation.2 | async-start | bytes 11796480 | tf_op jit(solution)/shard_map/all_to_all | solution.py:202
  300.4 13.9 %copy-start.3 = (s32[128]{0:T(128)S(1)}, s32[128]{0:T(128)}, u32[]{:S(2)}) copy-start(s32[128]{0:T(128)} %param.7) | copy-start | bytes 1540
  300.4 13.9 %copy-start.2 = (f32[128,4,3,17]{0,1,3,2:T(4,128)S(1)}, f32[128,4,3,17]{0,1,3,2:T(4,128)}, u32[]{:S(2)}) copy-start(f32[128,4,3,17]{0,1,3,2:T(4,128)} %param.6) | copy-start | bytes 313348
  314.8 14.5 %slice-start.2 = ((s8[4521984]{0:T(1024)(128)(4,1)}), s8[4194304]{0:T(1024)(128)(4,1)S(1)}, s32[]{:S(2)}) async-start(s8[4521984]{0:T(1024)(128)(4,1)} %bitcast.19), calls=%async_computation.6 | async-start | bytes 8388608
  321.6 7.7 %slice-start.3 = ((s8[4521984]{0:T(1024)(128)(4,1)}), s8[327680]{0:T(1024)(128)(4,1)S(1)}, s32[]{:S(2)}) async-start(s8[4521984]{0:T(1024)(128)(4,1)} %bitcast.19), calls=%async_computation.7 | async-start | bytes 655360
  322.6 33.6 %collective-permute-start.2 = (bf16[1,208,256]{2,1,0:T(8,128)(2,1)S(1)}, bf16[1,208,256]{2,1,0:T(8,128)(2,1)S(1)}, u32[]{:S(2)}, u32[]{:S(2)}) collective-permute-start(bf16[1,208,256]{2,1,0:T(8,128)(2,1)S(1)} %get-tuple-element.23), channel_id=1, source_target_pairs={{0,8},{8,16},{16,24},{1,9},{9,17},{17,25},{2,10},{10,18},{18,26},{... | collective-permute-start | bytes 319496 | tf_op jit(solution)/shard_map/ppermute | solution.py:27
  327.1 29.0 %collective-permute-start.3 = (bf16[1,208,256]{2,1,0:T(8,128)(2,1)S(1)}, bf16[1,208,256]{2,1,0:T(8,128)(2,1)S(1)}, u32[]{:S(2)}, u32[]{:S(2)}) collective-permute-start(bf16[1,208,256]{2,1,0:T(8,128)(2,1)S(1)} %get-tuple-element.24), channel_id=1, source_target_pairs={{8,0},{16,8},{24,16},{9,1},{17,9},{25,17},{10,2},{18,10},{26,18},{... | collective-permute-start | bytes 319496 | tf_op jit(solution)/shard_map/ppermute | solution.py:30
  356.2 15.2 %copy-start.1 = (bf16[4,256,256]{2,1,0:T(8,128)(2,1)S(1)}, bf16[4,256,256]{2,1,0:T(8,128)(2,1)}, u32[]{:S(2)}) copy-start(bf16[4,256,256]{2,1,0:T(8,128)(2,1)} %mix_ref.1) | copy-start | bytes 1572868
  356.2 55.5 %slice-start.4 = ((s8[6029312]{0:T(1024)(128)(4,1)}), s8[1835008]{0:T(1024)(128)(4,1)S(1)}, s32[]{:S(2)}) async-start(s8[6029312]{0:T(1024)(128)(4,1)} %bitcast.25), calls=%async_computation.8 | async-start | bytes 3670016
  371.4 40.3 %slice-start.5 = ((s8[6029312]{0:T(1024)(128)(4,1)}), s8[4194304]{0:T(1024)(128)(4,1)S(1)}, s32[]{:S(2)}) async-start(s8[6029312]{0:T(1024)(128)(4,1)} %bitcast.25), calls=%async_computation.9 | async-start | bytes 8388608
  427.6 135.6 %all-to-all-start.3 = ((bf16[8,8,180,256]{3,1,2,0:T(8,128)(2,1)}), bf16[8,8,180,256]{3,1,2,0:T(8,128)(2,1)}, u32[]{:S(2)}, u32[]{:S(2)}) async-start(bf16[8,8,180,256]{3,1,2,0:T(8,128)(2,1)} %copy.42), calls=%async_computation.3 | async-start | bytes 11796480 | tf_op jit(solution)/shard_map/all_to_all | solution.py:202

commit v3 on v2

--- a/solution.py
+++ b/solution.py
@@ -201,7 +201,8 @@
     def swap(piece):
         return lax.all_to_all(piece, "lon", split_axis=0, concat_axis=0, tiled=True)
 
-    gathered = [swap(split[:, q]) for q in range(PARTS)]
+    head, split = lax.optimization_barrier((split[:, 0], split))
+    gathered = [swap(head)] + [swap(split[:, q]) for q in range(1, PARTS)]
     first, forward, adjoint = lax.optimization_barrier((gathered[0], *tables(count, cols)))
     results = [transform(piece, forward, adjoint, gains) for piece in [first] + gathered[1:]]
     near, _ = lax.optimization_barrier((fields, first))

time: 580 us -> 576 us (level)
    squeeze x3, local copies, waits for them, and re-layouts: 16.4 us -> 9.29 us  [the longest x2 6.09 us: shards(): gathered = [swap(head)] + [swap(split[:, q]) for q in range(1, PARTS)]]
where the time goes in v3:
time: 576 us; the launch traced here: 569 us
  waiting for transfers between devices  270 us (47%)
  Pallas kernels  114 us (20%)
  local copies, waits for them, and re-layouts  91.1 us (16%)
  other arithmetic  58 us (10%)
  starting transfers between devices  35.2 us (6%)
    all_to_all x4, waiting for transfers between devices, swap(): return lax.all_to_all(piece, 'lon', split_axis=0, concat_axis=0, tiled=True)  234 us
    pallas_call x2, Pallas kernels, transform(): pl.pallas_call(functools.partial(transform_kernel, count, cols, rows), gr...  53.7 us
    pallas_call x1, Pallas kernels, local_part(): pl.pallas_call(functools.partial(local_kernel, tiles), grid=(lat_rows //...  40.3 us
    ppermute x2, waiting for transfers between devices, exchange(): lax.ppermute(lax.slice_in_dim(block, 0, width, axis=dim), axis, backward)  35.6 us
    cos x1, other arithmetic, tables(): forward = jnp.concatenate([jnp.cos(angle), -jnp.sin(angle)], 1)  26.1 us
    all_to_all x4, starting transfers between devices, swap(): return lax.all_to_all(piece, 'lon', split_axis=0, concat_axis=0, tiled=True)  26.1 us
    unnamed x22, local copies, waits for them, and re-layouts  21.7 us
    pallas_call x2, Pallas kernels, add_part(): pl.pallas_call(add_kernel, grid=(steps,), in_specs=[wide, pl.BlockSpec((c...  20.4 us
  transfers between devices with their start and end apart: 8, of which 5 were waited for; matrix products, arithmetic and copies ran while one was open for 25% of the time, Pallas kernels for 18%

profile of v3, /device:TPU:13, one launch (start us, length us, event | category | flops | bytes accessed | tf_op | source)
XLA Modules:
  0.0 568.7 jit_solution(2158099818053468531)
XLA Ops:
  0.0 3.2 slice_bitcast_fusion
  3.2 3.0 copy.30
  6.2 5.7 all-to-all-start.1
  11.8 3.2 slice_bitcast_fusion.1
  15.0 2.9 copy.29
  17.9 121.1 %all-to-all-done.1 = bf16[8,8,180,256]{3,1,2,0:T(8,128)(2,1)} async-done(((bf16[8,8,180,256]{3,1,2,0:T(8,128)(2,1)}), bf16[8,8,180,256]{3,1,2,0:T(8,128)(2,1)}, u32[]{:S(2)}, u32[]{:S(2)}) %all-to-all-start.1) | async-done | bytes 5898272 | tf_op jit(solution)/shard_map/all_to_all | solution.py:202
  139.0 6.5 %all-to-all-start = ((bf16[8,8,180,256]{3,1,2,0:T(8,128)(2,1)}), bf16[8,8,180,256]{3,1,2,0:T(8,128)(2,1)}, u32[]{:S(2)}, u32[]{:S(2)}) async-start(bf16[8,8,180,256]{3,1,2,0:T(8,128)(2,1)} %copy.29), calls=%async_computation | async-start | bytes 11796480 | tf_op jit(solution)/shard_map/all_to_all | solution.py:202
  145.5 26.1 %fusion.6 = (f32[8,180,720]{1,2,0:T(8,128)}, f32[8,180,720]{1,2,0:T(8,128)}) fusion(s32[8,180]{1,0:T(8,128)S(1)} %multiply_add_fusion), kind=kLoop, calls=%fused_computation.13 | loop fusion | flops 10368000 | bytes 8300160 | tf_op jit(solution)/shard_map/cos | solution.py:43
  171.7 7.8 %multiply_convert_fusion = bf16[8,180,1440]{1,2,0:T(8,128)(2,1)} fusion(f32[8,180,720]{1,2,0:T(8,128)} %get-tuple-element.32, f32[8,180,720]{1,2,0:T(8,128)} %get-tuple-element.31, f32[1440]{0:T(1024)S(1)} %pad_maximum_fusion.6), kind=kLoop, calls=%fused_computation.2 | loop fusion | flops 6220800 | bytes 12447360 | tf_op jit(solution)/shard_map/convert_element_type | solution.py:46
  179.5 7.8 %copy.43 = bf16[8,180,1440]{2,1,0:T(8,128)(2,1)} copy(bf16[8,180,1440]{1,2,0:T(8,128)(2,1)} %multiply_convert_fusion) | data formatting | bytes 8294400
  187.3 4.8 pad.15.clone
  192.1 7.6 %fusion.3.f_ref = bf16[8,1440,180]{2,1,0:T(8,128)(2,1)} fusion(f32[8,180,720]{1,2,0:T(8,128)} %get-tuple-element.32, f32[8,180,720]{1,2,0:T(8,128)} %get-tuple-element.31), kind=kLoop, calls=%fused_computation.7 | loop fusion | flops 8294400 | bytes 12441600 | tf_op jit(solution)/shard_map/transpose | solution.py:50
  199.7 6.7 %copy.33.x_ref = bf16[8,8,180,256]{3,2,1,0:T(8,128)(2,1)} copy(bf16[8,8,180,256]{3,1,2,0:T(8,128)(2,1)} %all-to-all-done.1) | data formatting | bytes 11796480 | tf_op jit(solution)/shard_map/optimization_barrier | solution.py:206
  206.4 12.1 %copy.34 = bf16[128,180,256]{2,1,0:T(8,128)(2,1)S(1)} copy(bf16[128,180,256]{2,0,1:T(8,128)(2,1)} %param.5) | data formatting | bytes 23592960 | tf_op jit(solution)/shard_map/optimization_barrier | solution.py:208
  221.1 26.9 %transform.3 = bf16[8,8,180,256]{3,2,1,0:T(8,128)(2,1)} custom-call(bf16[8,8,180,256]{3,2,1,0:T(8,128)(2,1)} %copy.33.x_ref, bf16[8,1440,180]{2,1,0:T(8,128)(2,1)} %fusion.3.f_ref, bf16[1472,1440]{1,0:T(8,128)(2,1)S(1)} %bitcast.18, f32[2,720,256]{2,1,0:T(8,128)S(1)} %copy-done), custom_call_target="tpu_custom_call" | custom-call | flops 16986931200 | bytes 23796480 | tf_op jit(solution)/shard_map/transform/pallas_call | solution.py:79
  248.0 35.6 %collective-permute-done.1 = bf16[128,8,256]{2,1,0:T(8,128)(2,1)S(1)} collective-permute-done((bf16[128,8,256]{2,1,0:T(8,128)(2,1)S(1)}, bf16[128,8,256]{2,1,0:T(8,128)(2,1)S(1)}, u32[]{:S(2)}, u32[]{:S(2)}) %collective-permute-start.1) | collective-permute-done | bytes 524320 | tf_op jit(solution)/shard_map/ppermute | solution.py:30
  283.8 6.4 %copy.41 = bf16[8,8,180,256]{3,1,2,0:T(8,128)(2,1)} copy(bf16[8,8,180,256]{3,2,1,0:T(8,128)(2,1)} %transform.3) | data formatting | bytes 11796480 | tf_op jit(solution)/shard_map/optimization_barrier | solution.py:210
  290.2 5.6 all-to-all-start.2
  295.8 13.8 %copy.36.x_ref = bf16[128,180,256]{2,1,0:T(8,128)(2,1)} copy(bf16[128,180,256]{2,0,1:T(8,128)(2,1)} %param.5) | data formatting | bytes 23592960 | tf_op args[0]
  310.0 6.7 %copy.32.x_ref = bf16[8,8,180,256]{3,2,1,0:T(8,128)(2,1)} copy(bf16[8,8,180,256]{3,1,2,0:T(8,128)(2,1)} %all-to-all-done) | data formatting | bytes 11796480 | tf_op jit(solution)/shard_map/all_to_all | solution.py:202
  317.9 4.6 collective-permute-start.2
  322.4 2.1 collective-permute-start.3
  324.6 26.9 %transform.2 = bf16[8,8,180,256]{3,2,1,0:T(8,128)(2,1)} custom-call(bf16[8,8,180,256]{3,2,1,0:T(8,128)(2,1)} %copy.32.x_ref, bf16[8,1440,180]{2,1,0:T(8,128)(2,1)} %fusion.3.f_ref, bf16[1472,1440]{1,0:T(8,128)(2,1)S(1)} %bitcast.21, f32[2,720,256]{2,1,0:T(8,128)S(1)} %copy-done), custom_call_target="tpu_custom_call" | custom-call | flops 16986931200 | bytes 23796480 | tf_op jit(solution)/shard_map/transform/pallas_call | solution.py:79
  351.5 15.2 %pad_maximum_fusion.w_ref.n0_ref.n1_ref = bf16[130,208,256]{2,1,0:T(8,128)(2,1)} fusion(bf16[1,208,256]{2,1,0:T(8,128)(2,1)S(1)} %collective-permute-done.3, bf16[128,12,256]{2,1,0:T(8,128)(2,1)S(1)} %broadcast_in_dim.19, bf16[128,8,256]{2,1,0:T(8,128)(2,1)S(1)} %collective-permute-done.1, bf16[128,180,256]{2,1,0:T(8,128)(2,1)} %copy.36.x_ref, ...), kind=kLoop, calls=%fused_computation | loop fusion | flops 83066880 | bytes 27688960 | tf_op jit(solution)/shard_map/concatenate | solution.py:216
  366.7 40.3 %local.1 = bf16[128,180,256]{2,1,0:T(8,128)(2,1)} custom-call(bf16[130,208,256]{2,1,0:T(8,128)(2,1)} %pad_maximum_fusion.w_ref.n0_ref.n1_ref, bf16[130,208,256]{2,1,0:T(8,128)(2,1)} %pad_maximum_fusion.w_ref.n0_ref.n1_ref, bf16[130,208,256]{2,1,0:T(8,128)(2,1)} %pad_maximum_fusion.w_ref.n0_ref.n1_ref, f32[128,4,256]{2,1,0:T(4,128)S(1)} %pad_convert_fusion.taps_ref, ...), custom_call_target="tpu_custom_call" | custom-call | flops 25769803776 | bytes 55377920 | tf_op jit(solution)/shard_map/local/pallas_call | solution.py:142
  407.0 3.8 copy.42
  410.8 12.1 %all-to-all-done.2 = bf16[8,8,180,256]{3,1,2,0:T(8,128)(2,1)} async-done(((bf16[8,8,180,256]{3,1,2,0:T(8,128)(2,1)}), bf16[8,8,180,256]{3,1,2,0:T(8,128)(2,1)}, u32[]{:S(2)}, u32[]{:S(2)}) %all-to-all-start.2) | async-done | bytes 5898272 | tf_op jit(solution)/shard_map/all_to_all | solution.py:202
  422.9 8.4 %all-to-all-start.3 = ((bf16[8,8,180,256]{3,1,2,0:T(8,128)(2,1)}), bf16[8,8,180,256]{3,1,2,0:T(8,128)(2,1)}, u32[]{:S(2)}, u32[]{:S(2)}) async-start(bf16[8,8,180,256]{3,1,2,0:T(8,128)(2,1)} %copy.42), calls=%async_computation.3 | async-start | bytes 11796480 | tf_op jit(solution)/shard_map/all_to_all | solution.py:202
  431.4 16.1 %copy.40 = bf16[180,128,256]{2,1,0:T(8,128)(2,1)} copy(bf16[180,128,256]{2,0,1:T(8,128)(2,1)} %bitcast.25) | data formatting | bytes 23592960 | tf_op jit(solution)/shard_map/transpose | solution.py:227
  447.5 10.2 %add.38.base_ref = bf16[180,8,2,8,256]{4,3,2,1,0:T(8,128)(2,1)} custom-call(bf16[180,8,2,8,256]{4,3,2,1,0:T(8,128)(2,1)} %bitcast.22, bf16[8,180,8,256]{3,2,1,0:T(8,128)(2,1)} %bitcast.8.back_ref), custom_call_target="tpu_custom_call", output_to_operand_aliasing={{}: (0, {})} | custom-call | flops 2949120 | bytes 17694720 | tf_op jit(solution)/shard_map/add/pallas_call | solution.py:177
  457.7 100.8 %all-to-all-done.3 = bf16[8,8,180,256]{3,1,2,0:T(8,128)(2,1)} async-done(((bf16[8,8,180,256]{3,1,2,0:T(8,128)(2,1)}), bf16[8,8,180,256]{3,1,2,0:T(8,128)(2,1)}, u32[]{:S(2)}, u32[]{:S(2)}) %all-to-all-start.3) | async-done | bytes 5898272 | tf_op jit(solution)/shard_map/all_to_all | solution.py:202
  558.5 10.2 %add.39 = bf16[180,8,2,8,256]{4,3,2,1,0:T(8,128)(2,1)} custom-call(bf16[180,8,2,8,256]{4,3,2,1,0:T(8,128)(2,1)} %add.38.base_ref, bf16[8,180,8,256]{3,2,1,0:T(8,128)(2,1)} %bitcast.9.back_ref), custom_call_target="tpu_custom_call", output_to_operand_aliasing={{}: (0, {})} | custom-call | flops 2949120 | bytes 17694720 | tf_op jit(solution)/shard_map/add/pallas_call | solution.py:177
  (41 shorter events, 4.5 us)
Async XLA Ops:
  6.2 132.8 %all-to-all-start.1 = ((bf16[8,8,180,256]{3,1,2,0:T(8,128)(2,1)}), bf16[8,8,180,256]{3,1,2,0:T(8,128)(2,1)}, u32[]{:S(2)}, u32[]{:S(2)}) async-start(bf16[8,8,180,256]{3,1,2,0:T(8,128)(2,1)} %copy.30), calls=%async_computation.1 | async-start | bytes 11796480 | tf_op jit(solution)/shard_map/all_to_all | solution.py:202
  139.0 151.2 %all-to-all-start = ((bf16[8,8,180,256]{3,1,2,0:T(8,128)(2,1)}), bf16[8,8,180,256]{3,1,2,0:T(8,128)(2,1)}, u32[]{:S(2)}, u32[]{:S(2)}) async-start(bf16[8,8,180,256]{3,1,2,0:T(8,128)(2,1)} %copy.29), calls=%async_computation | async-start | bytes 11796480 | tf_op jit(solution)/shard_map/all_to_all | solution.py:202
  199.7 21.4 %slice-start = ((s8[4521984]{0:T(1024)(128)(4,1)}), s8[4194304]{0:T(1024)(128)(4,1)S(1)}, s32[]{:S(2)}) async-start(s8[4521984]{0:T(1024)(128)(4,1)} %bitcast.16), calls=%async_computation.4 | async-start | bytes 8388608
  206.4 14.7 %slice-start.1 = ((s8[4521984]{0:T(1024)(128)(4,1)}), s8[327680]{0:T(1024)(128)(4,1)S(1)}, s32[]{:S(2)}) async-start(s8[4521984]{0:T(1024)(128)(4,1)} %bitcast.16), calls=%async_computation.5 | async-start | bytes 655360
  206.4 14.7 %copy-start = (f32[2,720,256]{2,1,0:T(8,128)S(1)}, f32[2,720,256]{2,1,0:T(8,128)}, u32[]{:S(2)}) copy-start(f32[2,720,256]{2,1,0:T(8,128)} %g_ref.3) | copy-start | bytes 4423684
  218.7 64.9 %collective-permute-start.1 = (bf16[128,8,256]{2,1,0:T(8,128)(2,1)S(1)}, bf16[128,8,256]{2,1,0:T(8,128)(2,1)S(1)}, u32[]{:S(2)}, u32[]{:S(2)}) collective-permute-start(bf16[128,8,256]{2,1,0:T(8,128)(2,1)S(1)} %get-tuple-element.29), channel_id=1, source_target_pairs={{1,0},{2,1},{3,2},{4,3},{5,4},{6,5},{7,6},{0,7},{9,8},{10,9},{11,1... | collective-permute-start | bytes 1572872 | tf_op jit(solution)/shard_map/ppermute | solution.py:30
  219.0 64.7 %collective-permute-start = (bf16[128,8,256]{2,1,0:T(8,128)(2,1)S(1)}, bf16[128,8,256]{2,1,0:T(8,128)(2,1)S(1)}, u32[]{:S(2)}, u32[]{:S(2)}) collective-permute-start(bf16[128,8,256]{2,1,0:T(8,128)(2,1)S(1)} %get-tuple-element.30), channel_id=1, source_target_pairs={{0,1},{1,2},{2,3},{3,4},{4,5},{5,6},{6,7},{7,0},{8,9},{9,10},{10,1... | collective-permute-start | bytes 1572872 | tf_op jit(solution)/shard_map/ppermute | solution.py:27
  290.2 132.7 %all-to-all-start.2 = ((bf16[8,8,180,256]{3,1,2,0:T(8,128)(2,1)}), bf16[8,8,180,256]{3,1,2,0:T(8,128)(2,1)}, u32[]{:S(2)}, u32[]{:S(2)}) async-start(bf16[8,8,180,256]{3,1,2,0:T(8,128)(2,1)} %copy.41), calls=%async_computation.2 | async-start | bytes 11796480 | tf_op jit(solution)/shard_map/all_to_all | solution.py:202
  295.8 13.8 %copy-start.3 = (s32[128]{0:T(128)S(1)}, s32[128]{0:T(128)}, u32[]{:S(2)}) copy-start(s32[128]{0:T(128)} %param.7) | copy-start | bytes 1540
  295.8 13.9 %copy-start.2 = (f32[128,4,3,17]{0,1,3,2:T(4,128)S(1)}, f32[128,4,3,17]{0,1,3,2:T(4,128)}, u32[]{:S(2)}) copy-start(f32[128,4,3,17]{0,1,3,2:T(4,128)} %param.6) | copy-start | bytes 313348
  310.0 14.5 %slice-start.2 = ((s8[4521984]{0:T(1024)(128)(4,1)}), s8[4194304]{0:T(1024)(128)(4,1)S(1)}, s32[]{:S(2)}) async-start(s8[4521984]{0:T(1024)(128)(4,1)} %bitcast.19), calls=%async_computation.6 | async-start | bytes 8388608
  316.8 7.8 %slice-start.3 = ((s8[4521984]{0:T(1024)(128)(4,1)}), s8[327680]{0:T(1024)(128)(4,1)S(1)}, s32[]{:S(2)}) async-start(s8[4521984]{0:T(1024)(128)(4,1)} %bitcast.19), calls=%async_computation.7 | async-start | bytes 655360
  317.9 33.6 %collective-permute-start.2 = (bf16[1,208,256]{2,1,0:T(8,128)(2,1)S(1)}, bf16[1,208,256]{2,1,0:T(8,128)(2,1)S(1)}, u32[]{:S(2)}, u32[]{:S(2)}) collective-permute-start(bf16[1,208,256]{2,1,0:T(8,128)(2,1)S(1)} %get-tuple-element.27), channel_id=1, source_target_pairs={{0,8},{8,16},{16,24},{1,9},{9,17},{17,25},{2,10},{10,18},{18,26},{... | collective-permute-start | bytes 319496 | tf_op jit(solution)/shard_map/ppermute | solution.py:27
  322.4 29.0 %collective-permute-start.3 = (bf16[1,208,256]{2,1,0:T(8,128)(2,1)S(1)}, bf16[1,208,256]{2,1,0:T(8,128)(2,1)S(1)}, u32[]{:S(2)}, u32[]{:S(2)}) collective-permute-start(bf16[1,208,256]{2,1,0:T(8,128)(2,1)S(1)} %get-tuple-element.28), channel_id=1, source_target_pairs={{8,0},{16,8},{24,16},{9,1},{17,9},{25,17},{10,2},{18,10},{26,18},{... | collective-permute-start | bytes 319496 | tf_op jit(solution)/shard_map/ppermute | solution.py:30
  351.5 15.2 %copy-start.1 = (bf16[4,256,256]{2,1,0:T(8,128)(2,1)S(1)}, bf16[4,256,256]{2,1,0:T(8,128)(2,1)}, u32[]{:S(2)}) copy-start(bf16[4,256,256]{2,1,0:T(8,128)(2,1)} %mix_ref.1) | copy-start | bytes 1572868
  351.5 55.5 %slice-start.4 = ((s8[6029312]{0:T(1024)(128)(4,1)}), s8[1835008]{0:T(1024)(128)(4,1)S(1)}, s32[]{:S(2)}) async-start(s8[6029312]{0:T(1024)(128)(4,1)} %bitcast.26), calls=%async_computation.8 | async-start | bytes 3670016
  366.7 40.3 %slice-start.5 = ((s8[6029312]{0:T(1024)(128)(4,1)}), s8[4194304]{0:T(1024)(128)(4,1)S(1)}, s32[]{:S(2)}) async-start(s8[6029312]{0:T(1024)(128)(4,1)} %bitcast.26), calls=%async_computation.9 | async-start | bytes 8388608
  422.9 135.6 %all-to-all-start.3 = ((bf16[8,8,180,256]{3,1,2,0:T(8,128)(2,1)}), bf16[8,8,180,256]{3,1,2,0:T(8,128)(2,1)}, u32[]{:S(2)}, u32[]{:S(2)}) async-start(bf16[8,8,180,256]{3,1,2,0:T(8,128)(2,1)} %copy.42), calls=%async_computation.3 | async-start | bytes 11796480 | tf_op jit(solution)/shard_map/all_to_all | solution.py:202
